TPU v7x, 128 devices: a whole 4x4x4 slice. The times are simulated.
128 devices in a mesh: expert: 32 (over y, z, x_hi), shard: 4 (over x_lo, core).
Axes of the slice: x: 4 (x_hi: 2, x_lo: 2; x = x_hi * 2 + x_lo), y: 4, z: 4, core: 2. Of those that a mesh axis runs over, the one named last changes fastest.
Arguments:
- tokens: bfloat16 [512, 4096], P('expert', 'shard'), may hold values from -6 to 6
- routes: int32 [512, 2], P('expert'), may hold values from 0 to 3, all different within a row
- gate_probs: float32 [512, 2], P('expert'), may hold values from 0.1 to 1
- prev_counts: int32 [4], replicated, may hold values from 32 to 192
- hosts: int32 [4], replicated, may hold values from 1 to 6
- w_gate: bfloat16 [32, 4096, 1536], P('expert', None, 'shard'), may hold values from -0.09375 to 0.09375
- w_up: bfloat16 [32, 4096, 1536], P('expert', None, 'shard'), may hold values from -0.09375 to 0.09375
- w_down: bfloat16 [32, 1536, 4096], P('expert', 'shard'), may hold values from -0.0546875 to 0.0546875
- grad_out: bfloat16 [512, 4096], P('expert', 'shard'), may hold values from -6 to 6
Outputs:
- outputs: bfloat16 [512, 4096], P('expert', 'shard')
- grad_tokens: bfloat16 [512, 4096], P('expert', 'shard')
- grad_gate: bfloat16 [32, 4096, 1536], P('expert', None, 'shard')
- grad_up: bfloat16 [32, 4096, 1536], P('expert', None, 'shard')
- grad_down: bfloat16 [32, 1536, 4096], P('expert', 'shard')
Inputs may be any that keep to these rules, and one draw needn't show every extreme that they name: `routes`: each token names two different experts.
All inputs are finite; a program needn't handle non-finite values.
Results may differ from a plain program's by a relative error of at most 0.0062.
Values may be sent and summed in bfloat16 or wider, within the bound.
No kernel may reach another device: no remote copies, remote signals or barrier semaphores. Data moves between devices by JAX's collectives and lax.ppermute only.
A program may use at most 192 MiB of HBM per device.

v0:
```python
import jax
import jax.numpy as jnp
from jax import lax
from jax.sharding import PartitionSpec as P

EXPERTS = 4
CAP = 6


HIGHEST_MODE = lax.Precision.HIGHEST


def partner_2(shard, axis, stride):
    return lax.ppermute(shard, axis, [(i, i ^ 1 << stride) for i in range(lax.axis_size(axis))])


def silu_parts(gate_vals):
    sigma = jax.nn.sigmoid(gate_vals)
    return (gate_vals * sigma, sigma * (1.0 + gate_vals * (1.0 - sigma)))


def assign_source(pair_experts, prev_counts, hosts, rank_count):
    count = pair_experts.shape[0]
    expert_ids = jnp.arange(EXPERTS, dtype=jnp.int32)
    partner = hosts.reshape(EXPERTS // 2, 2)[:, ::-1].reshape(EXPERTS)
    divisor = 2 * rank_count
    quota = jnp.minimum((prev_counts + divisor - 1) // divisor, CAP)
    onehot = pair_experts[:, None] == expert_ids[None, :]
    pair_quota = jnp.sum(jnp.where(onehot, quota[None, :], 0), axis=1, dtype=jnp.int32)
    pair_guest = jnp.sum(jnp.where(onehot, partner[None, :], 0), axis=1, dtype=jnp.int32)
    order_ids = jnp.arange(count, dtype=jnp.int32)
    earlier = order_ids[None, :] < order_ids[:, None]
    same = pair_experts[:, None] == pair_experts[None, :]
    position = jnp.sum(same & earlier, axis=1, dtype=jnp.int32)
    server = (position >= pair_quota).astype(jnp.int32)
    slot_row = position - server * pair_quota
    return (server, slot_row, position < pair_quota + pair_guest)


def matmul(left, right):
    return jnp.dot(left, right, preferred_element_type=jnp.float32)


def matmul_nt(left, right):
    return lax.dot_general(
        left, right, (((1,), (1,)), ((), ())), preferred_element_type=jnp.float32
    )


def matmul_tn(left, right):
    return lax.dot_general(
        left, right, (((0,), (0,)), ((), ())), preferred_element_type=jnp.float32
    )


def forward_block(block_rows, weights):
    gate_vals = matmul(block_rows, weights[0])
    up_vals = matmul(block_rows, weights[1])
    activation, slopes = silu_parts(gate_vals)
    hidden = (activation * up_vals).astype(jnp.bfloat16)
    return ((up_vals, activation, slopes, hidden), matmul(hidden, weights[2]))


def backward_block(block_rows, cotangent, stored, weights):
    up_vals, activation, slopes, hidden = stored
    d_hidden = matmul_nt(cotangent, weights[2])
    d_gate = (d_hidden * up_vals * slopes).astype(jnp.bfloat16)
    d_up = (d_hidden * activation).astype(jnp.bfloat16)
    d_rows = matmul_nt(d_gate, weights[0]) + matmul_nt(d_up, weights[1])
    return (
        d_rows,
        (matmul_tn(block_rows, d_gate), matmul_tn(block_rows, d_up), matmul_tn(hidden, cotangent)),
    )


def per_device(tokens, routes, gate_probs, prev_counts, hosts, w_gate, w_up, w_down, grad_out):
    rank_count = lax.axis_size("expert")
    group_size = rank_count // EXPERTS
    swap_bit = group_size.bit_length() - 1
    tok_rank = tokens.shape[0]
    pair_count = 2 * tok_rank
    slot_count = EXPERTS * 2 * CAP
    pair_experts = routes.reshape(pair_count)
    server, slot_row, kept_mask = assign_source(pair_experts, prev_counts, hosts, rank_count)
    target = jnp.where(server == 0, pair_experts, jnp.bitwise_xor(pair_experts, 1))
    position = (target * 2 + server) * CAP + slot_row
    slot_ids = jnp.arange(slot_count, dtype=jnp.int32)
    placed = ((position[:, None] == slot_ids[None, :]) & kept_mask[:, None]).astype(jnp.float32)
    pair_ids = jnp.arange(pair_count, dtype=jnp.int32) // 2
    owner_map = (pair_ids[:, None] == jnp.arange(tok_rank, dtype=jnp.int32)[None, :]).astype(
        jnp.float32
    )
    spread = jnp.dot(placed.T, owner_map, precision=HIGHEST_MODE)
    weighted = jnp.dot(
        placed.T, owner_map * gate_probs.reshape(pair_count, 1), precision=HIGHEST_MODE
    )

    def dispatch(slot_values):
        quarter = slot_values.shape[-1]
        blocks = slot_values.reshape(EXPERTS, 1, 2, CAP, quarter)
        copies = jnp.broadcast_to(blocks, (EXPERTS, group_size, 2, CAP, quarter)).reshape(
            rank_count, 2, CAP, quarter
        )
        arrived_part = lax.all_to_all(copies, "expert", split_axis=0, concat_axis=0, tiled=True)
        return lax.all_gather(arrived_part, "shard", axis=3, tiled=True)

    def collect(partial_value, combine):
        reduced = lax.psum_scatter(partial_value, "shard", scatter_dimension=3, tiled=True)
        returned_rows = lax.all_to_all(reduced, "expert", split_axis=0, concat_axis=0, tiled=True)
        per_slot = jnp.sum(
            returned_rows.reshape(EXPERTS, group_size, 2, CAP, returned_rows.shape[-1]), axis=1
        )
        return jnp.dot(combine.T, per_slot.reshape(slot_count, -1), precision=HIGHEST_MODE)

    own_weights = (w_gate[0], w_up[0], w_down[0])
    send_rows = jnp.dot(
        spread.astype(jnp.bfloat16), tokens, preferred_element_type=jnp.float32
    ).astype(jnp.bfloat16)
    arrived = dispatch(send_rows)
    feature_width = arrived.shape[-1]
    home_rows = arrived[:, 0].reshape(-1, feature_width)
    guest_rows = arrived[:, 1].reshape(-1, feature_width)
    swapped = partner_2((w_gate, w_up, w_down), "expert", swap_bit)
    other_weights = (swapped[0][0], swapped[1][0], swapped[2][0])
    home_saved, home_out = forward_block(home_rows, own_weights)
    work_saved, work_out = forward_block(guest_rows, other_weights)
    partial_out = jnp.stack(
        (home_out.reshape(rank_count, CAP, -1), work_out.reshape(rank_count, CAP, -1)), axis=1
    )
    outputs = collect(partial_out, weighted).astype(jnp.bfloat16)
    cot_send = jnp.dot(weighted, grad_out.astype(jnp.float32), precision=HIGHEST_MODE).astype(
        jnp.bfloat16
    )
    arrived_cot = dispatch(cot_send)
    home_cot = arrived_cot[:, 0].reshape(-1, feature_width)
    work_cot = arrived_cot[:, 1].reshape(-1, feature_width)
    home_back, home_grads = backward_block(home_rows, home_cot, home_saved, own_weights)
    work_back, work_grads = backward_block(guest_rows, work_cot, work_saved, other_weights)
    partial_back = jnp.stack(
        (home_back.reshape(rank_count, CAP, -1), work_back.reshape(rank_count, CAP, -1)), axis=1
    )
    grad_tokens = collect(partial_back, spread).astype(jnp.bfloat16)
    rounded_gate = work_grads[0].astype(jnp.bfloat16)
    rounded_up = work_grads[1].astype(jnp.bfloat16)
    rounded_down = work_grads[2].astype(jnp.bfloat16)
    returned = partner_2((rounded_gate, rounded_up, rounded_down), "expert", swap_bit)
    grad_gate = (home_grads[0] + returned[0].astype(jnp.float32)).astype(jnp.bfloat16)[None]
    grad_up = (home_grads[1] + returned[1].astype(jnp.float32)).astype(jnp.bfloat16)[None]
    grad_down = (home_grads[2] + returned[2].astype(jnp.float32)).astype(jnp.bfloat16)[None]
    return (outputs, grad_tokens, grad_gate, grad_up, grad_down)


def solution(mesh):
    placed = (
        P("expert", "shard"),
        P("expert", None),
        P("expert", None),
        P(),
        P(),
        P("expert", None, "shard"),
        P("expert", None, "shard"),
        P("expert", "shard", None),
        P("expert", "shard"),
    )
    return jax.shard_map(
        per_device,
        mesh=mesh,
        in_specs=placed,
        out_specs=(
            P("expert", "shard"),
            P("expert", "shard"),
            P("expert", None, "shard"),
            P("expert", None, "shard"),
            P("expert", "shard", None),
        ),
        check_vma=False,
    )
```

profile of v0, /device:TPU:0, one launch (start us, length us, event | category | flops | bytes accessed | tf_op | source)
XLA Modules:
  0.0 573.2 jit_solution(1150321479319378797)
XLA Ops:
  12.0 27.3 %all_to_all.20 = bf16[32,2,6,1024]{3,1,2,0:T(2,128)(2,1)} all-to-all(bf16[32,2,6,1024]{3,1,2,0:T(2,128)(2,1)S(1)} %bitcast.81), channel_id=1, replica_groups=mesh['expert'=32,'shard'=4] {'expert'}, dimensions={0} | all-to-all | bytes 1572864 | tf_op jit(solution)/shard_map/all_to_all | solution.py:104
  40.4 27.3 %all_to_all.21 = bf16[32,2,6,1024]{3,1,2,0:T(2,128)(2,1)} all-to-all(bf16[32,2,6,1024]{3,1,2,0:T(2,128)(2,1)S(1)} %bitcast.82), channel_id=1, replica_groups=mesh['expert'=32,'shard'=4] {'expert'}, dimensions={0} | all-to-all | bytes 1572864 | tf_op jit(solution)/shard_map/all_to_all | solution.py:104
  70.0 6.6 %all-gather.5.cloned.1.call-done = bf16[32,2,6,4096]{3,1,2,0:T(2,128)(2,1)} async-done(((bf16[32,2,6,1024]{3,1,2,0:T(2,128)(2,1)}), bf16[32,2,6,4096]{3,1,2,0:T(2,128)(2,1)}) %all-gather.5.cloned.1.call-update) | async-done | bytes 3145744 | tf_op jit(solution)/shard_map/all_gather | solution.py:105
  76.5 16.7 %slice_reduce_fusion.1 = (bf16[32,6,4096]{2,1,0:T(8,128)(2,1)}, bf16[32,6,4096]{2,1,0:T(8,128)(2,1)S(1)}) fusion(bf16[32,2,6,4096]{3,1,2,0:T(2,128)(2,1)} %all-gather.5.cloned.1.call-done), kind=kLoop, calls=%fused_computation.16 | loop fusion | bytes 6291456 | tf_op jit(solution)/shard_map/slice | solution.py:135
  94.7 23.1 %all-gather.3.cloned.1.call-done = bf16[32,2,6,4096]{3,1,2,0:T(2,128)(2,1)} async-done(((bf16[32,2,6,1024]{3,1,2,0:T(2,128)(2,1)}), bf16[32,2,6,4096]{3,1,2,0:T(2,128)(2,1)}) %all-gather.3.cloned.1.call-update) | async-done | bytes 3145744 | tf_op jit(solution)/shard_map/all_gather | solution.py:105
  117.8 17.4 %slice_reduce_fusion.3 = (bf16[32,6,4096]{2,1,0:T(8,128)(2,1)}, bf16[32,6,4096]{2,1,0:T(8,128)(2,1)}) fusion(bf16[32,2,6,4096]{3,1,2,0:T(2,128)(2,1)} %all-gather.3.cloned.1.call-done), kind=kLoop, calls=%fused_computation.18 | loop fusion | bytes 6291456 | tf_op jit(solution)/shard_map/slice | solution.py:121
  151.2 55.4 %collective-permute-done.1 = bf16[1,4096,384]{2,1,0:T(8,128)(2,1)} collective-permute-done((bf16[1,4096,384]{2,1,0:T(8,128)(2,1)}, bf16[1,4096,384]{2,1,0:T(8,128)(2,1)}, u32[]{:S(2)}, u32[]{:S(2)}) %collective-permute-start.1) | collective-permute-done | bytes 3145760 | tf_op jit(solution)/shard_map/ppermute | solution.py:14
  209.5 55.7 %collective-permute-done = bf16[1,4096,384]{2,1,0:T(8,128)(2,1)} collective-permute-done((bf16[1,4096,384]{2,1,0:T(8,128)(2,1)}, bf16[1,4096,384]{2,1,0:T(8,128)(2,1)}, u32[]{:S(2)}, u32[]{:S(2)}) %collective-permute-start) | collective-permute-done | bytes 3145760 | tf_op jit(solution)/shard_map/ppermute | solution.py:14
  273.3 4.4 multiply_convert_fusion.2
  290.8 5.7 convolution_add_fusion
  296.5 4.5 stack_reshape.9
  304.3 4.8 convolution_add_fusion.1
  309.1 4.3 stack_reshape.8
  313.4 8.3 %pad_maximum_fusion = f32[32,2,6,4096]{3,2,0,1:T(8,128)} fusion(f32[32,1,6,4096]{3,2,0,1:T(8,128)} %stack_reshape.9, f32[32,1,6,4096]{3,2,0,1:T(8,128)} %stack_reshape.8), kind=kLoop, calls=%fused_computation | loop fusion | flops 1572864 | bytes 12582912 | tf_op jit(solution)/shard_map/stack | solution.py:139
  321.7 4.2 convolution_convert_fusion
  333.9 11.7 %reduce-scatter.3.cloned.1.call-done = f32[32,2,6,1024]{3,0,2,1:T(8,128)} async-done(((f32[32,2,6,4096]{3,0,2,1:T(8,128)}), f32[32,2,6,1024]{3,0,2,1:T(8,128)}) %reduce-scatter.3.cloned.1.call-update) | async-done | bytes 1572880 | tf_op jit(solution)/shard_map/reduce_scatter | solution.py:108
  349.4 9.4 %all-to-all-start.1 = ((f32[32,2,6,1024]{3,1,2,0:T(2,128)}), f32[32,2,6,1024]{3,1,2,0:T(2,128)S(1)}, u32[]{:S(2)}, u32[]{:S(2)}) async-start(f32[32,2,6,1024]{3,1,2,0:T(2,128)} %copy.53), calls=%async_computation.2 | async-start | bytes 3145728 | tf_op jit(solution)/shard_map/all_to_all | solution.py:109
  358.9 86.0 %reduce-scatter.5.cloned.1.call-done = f32[32,2,6,1024]{3,2,0,1:T(8,128)} async-done(((f32[32,2,6,4096]{3,2,0,1:T(8,128)}), f32[32,2,6,1024]{3,2,0,1:T(8,128)}) %reduce-scatter.5.cloned.1.call-update) | async-done | bytes 1572880 | tf_op jit(solution)/shard_map/reduce_scatter | solution.py:108
  444.9 4.0 copy.57
  448.9 91.2 %all-to-all-done.1 = f32[32,2,6,1024]{3,1,2,0:T(2,128)S(1)} async-done(((f32[32,2,6,1024]{3,1,2,0:T(2,128)}), f32[32,2,6,1024]{3,1,2,0:T(2,128)S(1)}, u32[]{:S(2)}, u32[]{:S(2)}) %all-to-all-start.1) | async-done | bytes 1572896 | tf_op jit(solution)/shard_map/all_to_all | solution.py:109
  540.1 5.5 all-to-all-start.3
  545.6 5.1 fusion.2
  550.7 4.9 fusion
  555.6 4.9 fusion.1
  (90 shorter events, 70.5 us)
Async XLA Ops:
  7.2 3.9 copy-start
  7.2 32.4 %copy-start.10 = (bf16[16,1024]{1,0:T(8,128)(2,1)S(1)}, bf16[16,1024]{1,0:T(8,128)(2,1)}, u32[]{:S(2)}) copy-start(bf16[16,1024]{1,0:T(8,128)(2,1)} %param.9) | copy-start | bytes 98308
  7.2 69.3 %all-gather.5.cloned.1.call-start = ((), (), s32[]{:S(2)}) async-start(), calls=%async_computation.8 | async-start | bytes 3932160 | tf_op jit(solution)/shard_map/all_gather | solution.py:105
  39.3 78.5 %all-gather.3.cloned.1.call-start = ((), (), s32[]{:S(2)}) async-start(), calls=%async_computation.6 | async-start | bytes 3932160 | tf_op jit(solution)/shard_map/all_gather | solution.py:105
  67.7 277.9 %reduce-scatter.3.cloned.1.call-start = ((), (), s32[]{:S(2)}) async-start(), calls=%async_computation.7 | async-start | bytes 7864320 | tf_op jit(solution)/shard_map/reduce_scatter | solution.py:108
  67.8 80.3 %collective-permute-start.2 = (bf16[1,384,4096]{2,1,0:T(8,128)(2,1)}, bf16[1,384,4096]{2,1,0:T(8,128)(2,1)}, u32[]{:S(2)}, u32[]{:S(2)}) collective-permute-start(bf16[1,384,4096]{2,1,0:T(8,128)(2,1)} %param.16), channel_id=1, source_target_pairs={{0,32},{4,36},{8,40},{12,44},{16,48},{20,52},{24,56},{28,60},{32,0... | collective-permute-start | bytes 9437192 | tf_op jit(solution)/shard_map/ppermute | solution.py:14
  67.9 138.8 %collective-permute-start.1 = (bf16[1,4096,384]{2,1,0:T(8,128)(2,1)}, bf16[1,4096,384]{2,1,0:T(8,128)(2,1)}, u32[]{:S(2)}, u32[]{:S(2)}) collective-permute-start(bf16[1,4096,384]{2,1,0:T(8,128)(2,1)} %param.15), channel_id=1, source_target_pairs={{0,32},{4,36},{8,40},{12,44},{16,48},{20,52},{24,56},{28,60},{32,0... | collective-permute-start | bytes 9437192 | tf_op jit(solution)/shard_map/ppermute | solution.py:14
  69.9 195.4 %collective-permute-start = (bf16[1,4096,384]{2,1,0:T(8,128)(2,1)}, bf16[1,4096,384]{2,1,0:T(8,128)(2,1)}, u32[]{:S(2)}, u32[]{:S(2)}) collective-permute-start(bf16[1,4096,384]{2,1,0:T(8,128)(2,1)} %param.14), channel_id=1, source_target_pairs={{0,32},{4,36},{8,40},{12,44},{16,48},{20,52},{24,56},{28,60},{32,0... | collective-permute-start | bytes 9437192 | tf_op jit(solution)/shard_map/ppermute | solution.py:14
  144.4 3.7 copy-start.2
  278.5 3.0 copy-start.3
  287.5 157.3 %reduce-scatter.5.cloned.1.call-start = ((), (), s32[]{:S(2)}) async-start(), calls=%async_computation.9 | async-start | bytes 10485760 | tf_op jit(solution)/shard_map/reduce_scatter | solution.py:108
  287.6 3.3 copy-start.8
  301.1 3.3 copy-start.6
  321.7 4.2 copy-start.9
  325.9 5.0 copy-start.5
  325.9 219.7 %collective-permute-start.5 = (bf16[384,4096]{1,0:T(8,128)(2,1)}, bf16[384,4096]{1,0:T(8,128)(2,1)}, u32[]{:S(2)}, u32[]{:S(2)}) collective-permute-start(bf16[384,4096]{1,0:T(8,128)(2,1)} %convolution_convert_fusion), channel_id=1, source_target_pairs={{0,32},{4,36},{8,40},{12,44},{16,48},{20,52},{24,56},{28,60},{32,0... | collective-permute-start | bytes 9437192 | tf_op jit(solution)/shard_map/ppermute | solution.py:14
  328.9 221.8 %collective-permute-start.3 = (bf16[4096,384]{1,0:T(8,128)(2,1)}, bf16[4096,384]{1,0:T(8,128)(2,1)}, u32[]{:S(2)}, u32[]{:S(2)}) collective-permute-start(bf16[4096,384]{1,0:T(8,128)(2,1)} %convolution_convert_fusion.2), channel_id=1, source_target_pairs={{0,32},{4,36},{8,40},{12,44},{16,48},{20,52},{24,56},{28,60},{32,0... | collective-permute-start | bytes 9437192 | tf_op jit(solution)/shard_map/ppermute | solution.py:14
  333.9 221.6 %collective-permute-start.4 = (bf16[4096,384]{1,0:T(8,128)(2,1)}, bf16[4096,384]{1,0:T(8,128)(2,1)}, u32[]{:S(2)}, u32[]{:S(2)}) collective-permute-start(bf16[4096,384]{1,0:T(8,128)(2,1)} %convolution_convert_fusion.1), channel_id=1, source_target_pairs={{0,32},{4,36},{8,40},{12,44},{16,48},{20,52},{24,56},{28,60},{32,0... | collective-permute-start | bytes 9437192 | tf_op jit(solution)/shard_map/ppermute | solution.py:14
  349.4 190.7 %all-to-all-start.1 = ((f32[32,2,6,1024]{3,1,2,0:T(2,128)}), f32[32,2,6,1024]{3,1,2,0:T(2,128)S(1)}, u32[]{:S(2)}, u32[]{:S(2)}) async-start(f32[32,2,6,1024]{3,1,2,0:T(2,128)} %copy.53), calls=%async_computation.2 | async-start | bytes 3145728 | tf_op jit(solution)/shard_map/all_to_all | solution.py:109
  540.1 23.4 %all-to-all-start.3 = ((f32[32,2,6,1024]{3,1,2,0:T(2,128)}), f32[32,2,6,1024]{3,1,2,0:T(2,128)}, u32[]{:S(2)}, u32[]{:S(2)}) async-start(f32[32,2,6,1024]{3,1,2,0:T(2,128)} %copy.57), calls=%async_computation.5 | async-start | bytes 3145728 | tf_op jit(solution)/shard_map/all_to_all | solution.py:109
  545.6 5.1 copy-start.4
  550.7 4.9 copy-start.7
  555.6 10.8 %copy-start.1 = (bf16[16,1024]{1,0:T(8,128)(2,1)S(1)}, bf16[16,1024]{1,0:T(8,128)(2,1)}, u32[]{:S(2)}) copy-start(bf16[16,1024]{1,0:T(8,128)(2,1)} %param.17) | copy-start | bytes 98308
Sparse Core Ops, SparseCore 0:
  39.4 37.0 all-gather.4
  78.2 39.5 all-gather.2
  287.6 57.9 reduce-scatter.2
  347.9 96.8 reduce-scatter.4
where the time goes:
time: 582 us; the launch traced here: 573 us
  waiting for transfers between devices  331 us (57%)
  matrix products  71.8 us (12%)
  local copies, waits for them, and re-layouts  67 us (12%)
  blocking collectives  54.6 us (9%)
  starting transfers between devices  19.3 us (3%)
  other arithmetic  14.7 us (3%)
  between operations  14.3 us (2%)
    ppermute x6, waiting for transfers between devices, partner_2(): lax.ppermute(shard, axis, [(i, i ^ 1 << stride) for i in range(lax.axis_s...  111 us
    reduce_scatter x2, waiting for transfers between devices, collect(): lax.psum_scatter(partial_value, 'shard', scatter_dimension=3, tiled=True)  97.7 us
    all_to_all x2, waiting for transfers between devices, collect(): lax.all_to_all(reduced, 'expert', split_axis=0, concat_axis=0, tiled=True)  92.9 us
    all_to_all x2, blocking collectives, dispatch(): lax.all_to_all(copies, 'expert', split_axis=0, concat_axis=0, tiled=True)  54.6 us
    all_gather x2, waiting for transfers between devices, dispatch(): return lax.all_gather(arrived_part, 'shard', axis=3, tiled=True)  29.7 us
    dot_general x6, matrix products, matmul_tn(): lax.dot_general(left, right, (((0,), (0,)), ((), ())), preferred_element_...  25 us
    dot_general x6, matrix products, matmul_nt(): lax.dot_general(left, right, (((1,), (1,)), ((), ())), preferred_element_...  24.5 us
    dot_general x6, matrix products, matmul(): return jnp.dot(left, right, preferred_element_type=jnp.float32)  19.7 us
  transfers between devices with their start and end apart: 12, of which 8 were waited for; matrix products, arithmetic and copies ran while one was open for 22% of the time, Pallas kernels for 0%

commit v1 on v0

v1 whole, which is shorter than its diff:
```python
import jax
import jax.numpy as jnp
from jax import lax
from jax.experimental import pallas as pl
from jax.experimental.pallas import tpu as pltpu
from jax.sharding import PartitionSpec as P

AXES = ("expert", "shard")
EXPERTS = 4
CAP = 6
SLOTS = 12
PAIR = 2 * SLOTS
TOK = 16
BLOCK = 4 * SLOTS
ROWS = 8 * BLOCK
WIDTH = 1024
UNITS = 384
BF16 = jnp.bfloat16
F32 = jnp.float32
MIB = 1 << 20

VMEM = pl.BlockSpec(memory_space=pltpu.VMEM)
HBM = pl.BlockSpec(memory_space=pltpu.HBM)
NT = (((1,), (1,)), ((), ()))
TN = (((0,), (0,)), ((), ()))


def send(value, flip):
    return lax.ppermute(value, AXES, [(i, flip(i)) for i in range(128)])


def over_core(value):
    return send(value, lambda i: i ^ 1)


def over_y(value, mask):
    return send(value, lambda i: i ^ (mask << 5))


def over_first(value, mask):
    return send(value, lambda i: i ^ (mask << (3 if i & 1 else 1)))


def over_second(value, mask):
    return send(value, lambda i: i ^ (mask << (1 if i & 1 else 3)))


def exchange(values, over):
    return [values[0]] + [over(values[m], m) for m in (1, 2, 3)]


def call(kernel, name, specs, shapes, operands, mib=8, scratch=(), out=None):
    spaces = {id(VMEM): pltpu.VMEM, id(HBM): pltpu.HBM}
    operands = [
        pltpu.with_memory_space_constraint(x, spaces[id(spec)]) if id(spec) in spaces else x
        for spec, x in zip(specs, operands)
    ]
    return pl.pallas_call(
        kernel,
        out_shape=[jax.ShapeDtypeStruct(s, d) if out else pltpu.VMEM(s, d) for s, d in shapes],
        in_specs=specs,
        out_specs=[out or VMEM] * len(shapes),
        scratch_shapes=list(scratch),
        compiler_params=pltpu.CompilerParams(vmem_limit_bytes=mib * MIB),
        cost_estimate=pl.CostEstimate(flops=0, bytes_accessed=0, transcendentals=0),
        name=name,
    )(*operands)


def slots_of(counts, hosted, picks, gates):
    shape = (4 * PAIR, 2 * TOK)
    row = lax.broadcasted_iota(jnp.int32, shape, 0)
    lane = lax.broadcasted_iota(jnp.int32, shape, 1)
    mask = row // PAIR
    slot = row - mask * PAIR
    expert = jnp.bitwise_xor(mask, lax.axis_index("expert") // 8)
    a = lax.broadcasted_iota(jnp.int32, (2 * TOK, 2 * TOK), 0)
    b = lax.broadcasted_iota(jnp.int32, (2 * TOK, 2 * TOK), 1)
    earlier = jnp.where((a // TOK == b // TOK) & (a < b), 1.0, 0.0)
    late = slot >= SLOTS
    wanted = jnp.where(late, slot - SLOTS, slot)
    picked = jnp.concatenate([picks, picks], axis=1)
    probs = jnp.concatenate([gates, gates], axis=1)
    first = picked[0:1] == expert
    second = picked[1:2] == expert
    has = jnp.where(first | second, 1.0, 0.0)
    weight = jnp.where(first, probs[0:1], 0.0) + jnp.where(second, probs[1:2], 0.0)
    position = jnp.dot(has.astype(BF16), earlier.astype(BF16), preferred_element_type=F32)
    position = position.astype(jnp.int32)
    limit = jnp.zeros(shape, jnp.int32)
    for e in range(EXPERTS):
        quota = jnp.minimum((counts[e] + 63) // 64, CAP)
        limit = jnp.where(expert == e, quota + hosted[e ^ 1], limit)
    hit = (has > 0.5) & (position < limit) & (position == wanted) & (late == (lane >= TOK))
    return jnp.where(hit, 1.0, 0.0), late, weight


ROUTING = [
    pltpu.SMEM((EXPERTS,), jnp.int32),
    pltpu.SMEM((EXPERTS,), jnp.int32),
    pltpu.VMEM((2, TOK), jnp.int32),
    pltpu.VMEM((2, TOK), F32),
]


def fetch(sources, targets, sems):
    copies = [pltpu.make_async_copy(s, t, sems.at[i]) for i, (s, t) in enumerate(zip(sources, targets))]
    for copy in copies:
        copy.start()
    return copies


def pack(routing, tokens, grad_out):
    def kernel(*refs):
        sources, outs, (counts, hosted, picks, gates, values, sems) = refs[:6], refs[6:10], refs[10:]
        targets = [counts, hosted, picks, gates, values.at[:TOK], values.at[TOK:]]
        for copy in fetch(sources, targets, sems):
            copy.wait()
        one_hot, late, weight = slots_of(counts, hosted, picks[...], gates[...])
        scale = jnp.sum(jnp.where(late, one_hot * weight, one_hot), axis=1, keepdims=True)
        rows = jnp.dot(one_hot.astype(BF16), values[...], preferred_element_type=F32) * scale
        for m in range(4):
            outs[m][...] = rows[m * PAIR : (m + 1) * PAIR].astype(BF16)

    scratch = ROUTING + [pltpu.VMEM((2 * TOK, WIDTH), BF16), pltpu.SemaphoreType.DMA((6,))]
    shapes = [((PAIR, WIDTH), BF16)] * 4
    return call(kernel, "pack", [HBM] * 6, shapes, (*routing, tokens, grad_out), scratch=scratch)


def combine_matrix(routing):
    def kernel(*refs):
        sources, out, targets, sems = refs[:4], refs[4], refs[5:9], refs[9]
        for copy in fetch(sources, targets, sems):
            copy.wait()
        counts, hosted, picks, gates = targets
        one_hot, late, weight = slots_of(counts, hosted, picks[...], gates[...])
        out[...] = jnp.where(late, one_hot, one_hot * weight)

    scratch = ROUTING + [pltpu.SemaphoreType.DMA((4,))]
    return call(kernel, "combine_matrix", [HBM] * 4, [((4 * PAIR, 2 * TOK), F32)], routing, scratch=scratch)[0]


def join_y(parts):
    total = 4 * PAIR

    def kernel(a, b, c, d, out):
        stacked = jnp.concatenate([p[...].astype(F32) for p in (a, b, c, d)], axis=0).astype(BF16)
        to = lax.broadcasted_iota(jnp.int32, (total, total), 0)
        come = lax.broadcasted_iota(jnp.int32, (total, total), 1)
        half = to // BLOCK
        inner = to - half * BLOCK
        source = inner // SLOTS
        wanted = source * PAIR + half * SLOTS + (inner - source * SLOTS)
        order = jnp.where(come == wanted, 1.0, 0.0).astype(BF16)
        out[...] = jnp.dot(order, stacked, preferred_element_type=F32).astype(BF16)

    return call(kernel, "join_y", [VMEM] * 4, [((total, WIDTH), BF16)], parts)[0]


def load_weights(w_gate, w_up, w_down):
    def kernel(wg, wu, wd, both, down, sems):
        targets = [both.at[:, :UNITS], both.at[:, UNITS:], down]
        for copy in fetch([wg.at[0], wu.at[0], wd.at[0]], targets, sems):
            copy.wait()

    shapes = [((4 * WIDTH, 2 * UNITS), BF16), ((UNITS, 4 * WIDTH), BF16)]
    scratch = [pltpu.SemaphoreType.DMA((3,))]
    return call(kernel, "load_weights", [HBM] * 3, shapes, (w_gate, w_up, w_down), scratch=scratch)


def join_first(parts):
    def kernel(a, b, c, d, out):
        for m, part in enumerate((a, b, c, d)):
            out[m] = part[...]

    return call(kernel, "join_first", [VMEM] * 4, [((4, 2 * BLOCK, WIDTH), BF16)], parts)[0]


def join_second(parts, half):
    def kernel(a, b, c, d, out):
        for m, part in enumerate((a, b, c, d)):
            out[m] = part[:, half * BLOCK : (half + 1) * BLOCK, :]

    return call(kernel, f"join_second_{half}", [VMEM] * 4, [((4, 4, BLOCK, WIDTH), BF16)], parts)[0]


def place(core, xlm, zm, xhm):
    xm = xhm * 2 + xlm
    return jnp.where(core == 0, zm, xm), jnp.where(core == 0, xm, zm)


def rows_of(core, xlm, pieces):
    blocks = [pieces[place(core, xlm, zm, xhm)] for zm in range(4) for xhm in range(2)]
    return jnp.concatenate(blocks, axis=0)


def scatter_rows(core, xlm, rows, out_ref):
    for zm in range(4):
        for xhm in range(2):
            row = (zm * 2 + xhm) * BLOCK
            out_ref[place(core, xlm, zm, xhm)] = rows[row : row + BLOCK].astype(out_ref.dtype)


def at(shard, fm):
    return pl.ds(pl.multiple_of(jnp.bitwise_xor(shard, fm) * WIDTH, WIDTH), WIDTH)


def forward(cm, pieces, w_both, before):
    def kernel(pieces, w, *refs):
        shard = lax.axis_index("shard")
        total, both_ref = None if before is None else refs[0][...], refs[0 if before is None else 1]
        for xlm in range(2):
            rows = rows_of((shard & 1) ^ cm, xlm, pieces)
            part = jnp.dot(rows, w[at(shard, xlm * 2 + cm), :], preferred_element_type=F32)
            total = part if total is None else total + part
        both_ref[...] = total
        if before is not None:
            gate = both_ref[:, :UNITS]
            refs[2][...] = (gate * jax.nn.sigmoid(gate) * both_ref[:, UNITS:]).astype(BF16)

    shapes = [((ROWS, 2 * UNITS), F32)]
    specs, operands = [VMEM, VMEM], (pieces, w_both)
    if before is not None:
        shapes, specs, operands = shapes + [((ROWS, UNITS), BF16)], specs + [VMEM], operands + (before,)
    return call(kernel, f"forward_{cm}", specs, shapes, operands, 8)


def out_rows(cm, hidden, w_down):
    def kernel(hidden, w, out_ref):
        shard = lax.axis_index("shard")
        for xlm in range(2):
            rows = jnp.dot(hidden[...], w[:, at(shard, xlm * 2 + cm)], preferred_element_type=F32)
            scatter_rows((shard & 1) ^ cm, xlm, rows, out_ref)

    shapes = [((4, 4, BLOCK, WIDTH), BF16)]
    return call(kernel, f"out_rows_{cm}", [VMEM, VMEM], shapes, (hidden, w_down))[0]


def backward_hidden(cm, pieces, w_down, before, both):
    def kernel(pieces, w, *refs):
        shard = lax.axis_index("shard")
        total = None if before is None else refs[0][...]
        for xlm in range(2):
            rows = rows_of((shard & 1) ^ cm, xlm, pieces)
            part = lax.dot_general(rows, w[:, at(shard, xlm * 2 + cm)], NT, preferred_element_type=F32)
            total = part if total is None else total + part
        if before is None:
            refs[0][...] = total
            return
        both_ref, d_ref = refs[1:]
        gate, up = both_ref[:, :UNITS], both_ref[:, UNITS:]
        sigma = jax.nn.sigmoid(gate)
        d_ref[:, :UNITS] = (total * up * (sigma * (1.0 + gate * (1.0 - sigma)))).astype(BF16)
        d_ref[:, UNITS:] = (total * (gate * sigma)).astype(BF16)

    name, specs, operands = f"backward_hidden_{cm}", [VMEM, VMEM], (pieces, w_down)
    if before is None:
        return call(kernel, name, specs, [((ROWS, UNITS), F32)], operands)[0]
    shapes = [((ROWS, 2 * UNITS), BF16)]
    return call(kernel, name, specs + [VMEM] * 2, shapes, operands + (before, both))[0]


def back_rows(cm, d_both, w_both):
    def kernel(d, w, out_ref):
        shard = lax.axis_index("shard")
        for xlm in range(2):
            rows = lax.dot_general(d[...], w[at(shard, xlm * 2 + cm), :], NT, preferred_element_type=F32)
            scatter_rows((shard & 1) ^ cm, xlm, rows, out_ref)

    shapes = [((4, 4, BLOCK, WIDTH), BF16)]
    return call(kernel, f"back_rows_{cm}", [VMEM, VMEM], shapes, (d_both, w_both))[0]


def gate_up_grads(x_pieces, d_both):
    def kernel(mine, theirs, d, gate_out, up_out, total, sems):
        shard = lax.axis_index("shard")
        copies = [None] * 4
        for fm in range(4):
            slot = fm % 2
            if fm >= 2:
                wait_all(copies[fm - 2])
            rows = rows_of((shard & 1) ^ (fm % 2), fm // 2, theirs if fm % 2 else mine)
            total[slot] = lax.dot_general(rows, d[...], TN, preferred_element_type=F32).astype(BF16)
            sources = [total.at[slot, :, :UNITS], total.at[slot, :, UNITS:]]
            targets = [gate_out.at[0, at(shard, fm), :], up_out.at[0, at(shard, fm), :]]
            copies[fm] = fetch(sources, targets, sems.at[slot])
        wait_all(copies[2])
        wait_all(copies[3])

    shapes = [((1, 4 * WIDTH, UNITS), BF16)] * 2
    scratch = [pltpu.VMEM((2, WIDTH, 2 * UNITS), BF16), pltpu.SemaphoreType.DMA((2, 2))]
    operands = (*x_pieces, d_both)
    return call(kernel, "gate_up_grads", [VMEM] * 3, shapes, operands, 12, scratch, HBM)


def down_grad(cot_pieces, hidden):
    def kernel(mine, theirs, hidden, out, total, sems):
        shard = lax.axis_index("shard")
        copies = [None] * 4
        for fm in range(4):
            slot = fm % 2
            if fm >= 2:
                wait_all(copies[fm - 2])
            rows = rows_of((shard & 1) ^ (fm % 2), fm // 2, theirs if fm % 2 else mine)
            total[slot] = lax.dot_general(hidden[...], rows, TN, preferred_element_type=F32).astype(BF16)
            copies[fm] = fetch([total.at[slot]], [out.at[0, :, at(shard, fm)]], sems.at[slot])
        wait_all(copies[2])
        wait_all(copies[3])

    shapes = [((1, UNITS, 4 * WIDTH), BF16)]
    scratch = [pltpu.VMEM((2, UNITS, WIDTH), BF16), pltpu.SemaphoreType.DMA((2, 1))]
    operands = (*cot_pieces, hidden)
    return call(kernel, "down_grad", [VMEM] * 3, shapes, operands, 10, scratch, HBM)[0]


def wait_all(copies):
    for copy in copies:
        copy.wait()


def sum_cores(mine, theirs):
    def kernel(a, b, *outs):
        for m in range(4):
            outs[m][...] = (a[m].astype(F32) + b[m].astype(F32)).astype(BF16)

    return call(kernel, "sum_cores", [VMEM] * 2, [((4, BLOCK, WIDTH), BF16)] * 4, (mine, theirs))


def sum_second(pieces):
    def kernel(a, b, c, d, *outs):
        for m in range(4):
            total = (a[m].astype(F32) + b[m].astype(F32)) + (c[m].astype(F32) + d[m].astype(F32))
            outs[m][...] = total.astype(outs[m].dtype)

    shapes = [((BLOCK, WIDTH), F32)] + [((BLOCK, WIDTH), BF16)] * 3
    return call(kernel, "sum_second", [VMEM] * 4, shapes, pieces)


def sum_second_both(blocks, pieces):
    def kernel(*refs):
        (a, b, c, d), outs = refs[4:8], refs[8:]
        for m in range(4):
            total = (a[m].astype(F32) + b[m].astype(F32)) + (c[m].astype(F32) + d[m].astype(F32))
            outs[m][:BLOCK, :] = refs[m][...]
            outs[m][BLOCK:, :] = total.astype(outs[m].dtype)

    shapes = [((2 * BLOCK, WIDTH), F32)] + [((2 * BLOCK, WIDTH), BF16)] * 3
    return call(kernel, "sum_second_both", [VMEM] * 8, shapes, (*blocks, *pieces))


def sum_first(blocks):
    def kernel(a, b, c, d, *outs):
        total = (a[...] + b[...].astype(F32)) + (c[...].astype(F32) + d[...].astype(F32))
        for m in range(4):
            for half in range(2):
                row = half * BLOCK + m * SLOTS
                outs[m][half * SLOTS : (half + 1) * SLOTS, :] = total[row : row + SLOTS]

    return call(kernel, "sum_first", [VMEM] * 4, [((PAIR, WIDTH), F32)] * 4, blocks)


def combine(matrix, parts):
    def kernel(matrix, a, b, c, d, outputs, grads):
        stacked = jnp.concatenate([p[...] for p in (a, b, c, d)], axis=0)
        total = lax.dot_general(
            matrix[...], stacked, TN, precision=lax.Precision.HIGHEST, preferred_element_type=F32
        )
        outputs[...] = total[:TOK].astype(BF16)
        grads[...] = total[TOK:].astype(BF16)

    return call(kernel, "combine", [VMEM] * 5, [((TOK, WIDTH), BF16)] * 2, (matrix, *parts), out=VMEM)


def per_device(tokens, routes, gate_probs, prev_counts, hosts, w_gate, w_up, w_down, grad_out):
    routing = (prev_counts, hosts, routes.T, gate_probs.T)
    tie = lax.optimization_barrier
    payload = exchange(pack(routing, tokens, grad_out), over_y)
    payload, matrix, (w_both, w_down) = tie(
        (payload, combine_matrix(routing), load_weights(w_gate, w_up, w_down))
    )
    both = join_first(exchange([join_y(payload)] * 4, over_first))
    both = exchange([both] * 4, over_second)
    x_mine = join_second(both, 0)
    x_theirs = over_core(x_mine)
    cot_mine = join_second(both, 1)
    cot_theirs = over_core(cot_mine)

    (part,) = forward(0, x_mine, w_both, None)
    back_part = backward_hidden(0, cot_mine, w_down, None, None)
    gate_up, hidden = forward(1, x_theirs, w_both, part)
    d_both = backward_hidden(1, cot_theirs, w_down, back_part, gate_up)
    back_theirs = over_core(back_rows(1, d_both, w_both))
    back_mine = back_rows(0, d_both, w_both)
    back_pieces = exchange(sum_cores(back_mine, back_theirs), over_second)
    out_theirs = over_core(out_rows(1, hidden, w_down))
    out_mine = out_rows(0, hidden, w_down)
    out_pieces = exchange(sum_cores(out_mine, out_theirs), over_second)
    grads = (
        *gate_up_grads((x_mine, x_theirs), d_both),
        down_grad((cot_mine, cot_theirs), hidden),
    )
    back_pieces, out_pieces, grads = tie((back_pieces, out_pieces, grads))
    blocks = exchange(sum_second_both(sum_second(out_pieces), back_pieces), over_first)
    parts = exchange(sum_first(blocks), over_y)
    outputs, grad_tokens = combine(matrix, parts)
    return outputs, grad_tokens, *grads


def solution(mesh):
    rows, weights = P("expert", "shard"), P("expert", None, "shard")
    down = P("expert", "shard", None)
    small = P("expert", None)
    return jax.shard_map(
        per_device,
        mesh=mesh,
        in_specs=(rows, small, small, P(), P(), weights, weights, down, rows),
        out_specs=(rows, rows, weights, weights, down),
        check_vma=False,
    )
```

time: 582 us -> 108 us (0.19); the launches traced: 573 us -> 108 us
  waiting for transfers between devices: 331 us -> 44.5 us
  matrix products: 71.8 us -> 0 us
  local copies, waits for them, and re-layouts: 67 us -> 0 us
  blocking collectives: 54.6 us -> 0 us
  Pallas kernels: 0 us -> 28 us
  starting transfers between devices: 19.3 us -> 34.7 us
  other arithmetic: 14.7 us -> 0 us
  between operations: 14.3 us -> 0.87 us
    reduce_scatter x2 -> x0, waiting for transfers between devices: 97.7 us -> none  [collect(): lax.psum_scatter(partial_value, 'shard', scatter_dimension=3, tiled=True)]
    all_to_all x2 -> x0, waiting for transfers between devices: 92.9 us -> none  [collect(): lax.all_to_all(reduced, 'expert', split_axis=0, concat_axis=0, tiled=True)]
    dot_general x24 -> x0, matrix products: 71.8 us -> none  [the longest x6 25 us: matmul_tn(): lax.dot_general(left, right, (((0,), (0,)), ((), ())), preferred_element_...]
    ppermute x6 -> x25, waiting for transfers between devices: 111 us -> 44.5 us  [send(): return lax.ppermute(value, AXES, [(i, flip(i)) for i in range(128)])]
    all_to_all x2 -> x0, blocking collectives: 54.6 us -> none  [dispatch(): lax.all_to_all(copies, 'expert', split_axis=0, concat_axis=0, tiled=True)]
    slice x2 -> x0, local copies, waits for them, and re-layouts: 34.2 us -> none  [the longest x1 17.4 us: per_device(): home_rows = arrived[:, 0].reshape(-1, feature_width)]
    ppermute x6 -> x25, starting transfers between devices: 4.23 us -> 34.7 us  [send(): return lax.ppermute(value, AXES, [(i, flip(i)) for i in range(128)])]
    all_gather x2 -> x0, waiting for transfers between devices: 29.7 us -> none  [dispatch(): return lax.all_gather(arrived_part, 'shard', axis=3, tiled=True)]
  transfers between devices with their start and end apart: 12 -> 25, of which waited for: 8 -> 13; matrix products, arithmetic and copies ran while one was open for 22% -> 0% of each run, Pallas kernels for 0% -> 23%
where the time goes in v1:
time: 108 us
  waiting for transfers between devices  44.5 us (41%)
  starting transfers between devices  34.7 us (32%)
  Pallas kernels  28 us (26%)
    ppermute x25, waiting for transfers between devices, send(): return lax.ppermute(value, AXES, [(i, flip(i)) for i in range(128)])  44.5 us
    ppermute x25, starting transfers between devices, send(): return lax.ppermute(value, AXES, [(i, flip(i)) for i in range(128)])  34.7 us
    pallas_call x23, Pallas kernels, call(): pl.pallas_call(kernel, out_shape=[jax.ShapeDtypeStruct(s, d) if out else...  28 us
  transfers between devices with their start and end apart: 25, of which 13 were waited for; matrix products, arithmetic and copies ran while one was open for 0% of the time, Pallas kernels for 23%

profile of v1, /device:TPU:0, one launch (start us, length us, event | category | flops | bytes accessed | tf_op | source)
XLA Modules:
  0.0 108.1 jit_solution(11104378411138974111)
XLA Ops:
  1.9 1.7 %collective-permute-start = (bf16[24,1024]{1,0:T(8,128)(2,1)S(1)}, bf16[24,1024]{1,0:T(8,128)(2,1)S(1)}, u32[]{:S(2)}, u32[]{:S(2)}) collective-permute-start(bf16[24,1024]{1,0:T(8,128)(2,1)S(1)} %get-tuple-element.56), channel_id=1, source_target_pairs={{0,32},{1,33},{2,34},{3,35},{4,36},{5,37},{6,38},{7,39},{8,40},{9,... | collective-permute-start | bytes 147464 | tf_op jit(solution)/shard_map/ppermute | solution.py:29
  3.6 2.9 %collective-permute-start.1 = (bf16[24,1024]{1,0:T(8,128)(2,1)S(1)}, bf16[24,1024]{1,0:T(8,128)(2,1)S(1)}, u32[]{:S(2)}, u32[]{:S(2)}) collective-permute-start(bf16[24,1024]{1,0:T(8,128)(2,1)S(1)} %get-tuple-element.57), channel_id=1, source_target_pairs={{0,64},{1,65},{2,66},{3,67},{4,68},{5,69},{6,70},{7,71},{8,72},{9,... | collective-permute-start | bytes 147464 | tf_op jit(solution)/shard_map/ppermute | solution.py:29
  7.6 3.8 %load_weights.1 = (bf16[4096,768]{1,0:T(8,128)(2,1)S(1)}, bf16[384,4096]{1,0:T(8,128)(2,1)S(1)}) custom-call(bf16[1,4096,384]{2,1,0:T(8,128)(2,1)} %wg.1, bf16[1,4096,384]{2,1,0:T(8,128)(2,1)} %wu.1, bf16[1,384,4096]{2,1,0:T(8,128)(2,1)} %wd.1), custom_call_target="tpu_custom_call" | custom-call | tf_op jit(solution)/shard_map/load_weights/pallas_call | solution.py:58
  12.1 2.8 %collective-permute-start.5 = (bf16[96,1024]{1,0:T(8,128)(2,1)S(1)}, bf16[96,1024]{1,0:T(8,128)(2,1)S(1)}, u32[]{:S(2)}, u32[]{:S(2)}) collective-permute-start(bf16[96,1024]{1,0:T(8,128)(2,1)S(1)} %join_y.1.a), channel_id=1, source_target_pairs={{0,6},{1,25},{2,4},{3,27},{4,2},{5,29},{6,0},{7,31},{8,14},{9,17},... | collective-permute-start | bytes 589832 | tf_op jit(solution)/shard_map/ppermute | solution.py:29
  16.2 4.0 %collective-permute-done.5.d = bf16[96,1024]{1,0:T(8,128)(2,1)S(1)} collective-permute-done((bf16[96,1024]{1,0:T(8,128)(2,1)S(1)}, bf16[96,1024]{1,0:T(8,128)(2,1)S(1)}, u32[]{:S(2)}, u32[]{:S(2)}) %collective-permute-start.5) | collective-permute-done | bytes 196640 | tf_op jit(solution)/shard_map/ppermute | solution.py:29
  20.2 1.9 %collective-permute-done.4.c = bf16[96,1024]{1,0:T(8,128)(2,1)S(1)} collective-permute-done((bf16[96,1024]{1,0:T(8,128)(2,1)S(1)}, bf16[96,1024]{1,0:T(8,128)(2,1)S(1)}, u32[]{:S(2)}, u32[]{:S(2)}) %collective-permute-start.4) | collective-permute-done | bytes 196640 | tf_op jit(solution)/shard_map/ppermute | solution.py:29
  22.1 4.1 %collective-permute-start.8 = (bf16[4,96,1024]{2,1,0:T(8,128)(2,1)S(1)}, bf16[4,96,1024]{2,1,0:T(8,128)(2,1)S(1)}, u32[]{:S(2)}, u32[]{:S(2)}) collective-permute-start(bf16[4,96,1024]{2,1,0:T(8,128)(2,1)S(1)} %join_first.1.a), channel_id=1, source_target_pairs={{0,24},{1,7},{2,26},{3,5},{4,28},{5,3},{6,30},{7,1},{8,16},{9,15},... | collective-permute-start | bytes 2359304 | tf_op jit(solution)/shard_map/ppermute | solution.py:29
  27.2 17.4 %collective-permute-done.8.d = bf16[4,96,1024]{2,1,0:T(8,128)(2,1)S(1)} collective-permute-done((bf16[4,96,1024]{2,1,0:T(8,128)(2,1)S(1)}, bf16[4,96,1024]{2,1,0:T(8,128)(2,1)S(1)}, u32[]{:S(2)}, u32[]{:S(2)}) %collective-permute-start.8) | collective-permute-done | bytes 786464 | tf_op jit(solution)/shard_map/ppermute | solution.py:29
  49.2 1.4 %forward_1.1 = (f32[384,768]{1,0:T(8,128)S(1)}, bf16[384,384]{1,0:T(8,128)(2,1)S(1)}) custom-call(bf16[4,4,48,1024]{3,2,1,0:T(8,128)(2,1)S(1)} %collective-permute-done.10.pieces.theirs, bf16[4096,768]{1,0:T(8,128)(2,1)S(1)} %get-tuple-element.67.w, f32[384,768]{1,0:T(8,128)S(1)} %forward_0.1.refs_0_), custom_call_target="tpu_custom_call" | custom-call | tf_op jit(solution)/shard_map/forward_1/pallas_call | solution.py:58
  53.9 1.4 %back_rows_1.1 = bf16[4,4,48,1024]{3,2,1,0:T(8,128)(2,1)S(1)} custom-call(bf16[384,768]{1,0:T(8,128)(2,1)S(1)} %backward_hidden_1.1.d, bf16[4096,768]{1,0:T(8,128)(2,1)S(1)} %get-tuple-element.67.w), custom_call_target="tpu_custom_call" | custom-call | tf_op jit(solution)/shard_map/back_rows_1/pallas_call | solution.py:58
  58.3 1.4 %back_rows_0.1.a = bf16[4,4,48,1024]{3,2,1,0:T(8,128)(2,1)S(1)} custom-call(bf16[384,768]{1,0:T(8,128)(2,1)S(1)} %backward_hidden_1.1.d, bf16[4096,768]{1,0:T(8,128)(2,1)S(1)} %get-tuple-element.67.w), custom_call_target="tpu_custom_call" | custom-call | tf_op jit(solution)/shard_map/back_rows_0/pallas_call | solution.py:58
  59.8 3.8 %collective-permute-start.17 = (bf16[4,48,1024]{2,1,0:T(8,128)(2,1)S(1)}, bf16[4,48,1024]{2,1,0:T(8,128)(2,1)S(1)}, u32[]{:S(2)}, u32[]{:S(2)}) collective-permute-start(bf16[4,48,1024]{2,1,0:T(8,128)(2,1)S(1)} %get-tuple-element.76), channel_id=1, source_target_pairs={{0,16},{1,5},{2,18},{3,7},{4,20},{5,1},{6,22},{7,3},{8,24},{9,13},... | collective-permute-start | bytes 1179656 | tf_op jit(solution)/shard_map/ppermute | solution.py:29
  64.1 4.6 %collective-permute-start.13 = (bf16[4,48,1024]{2,1,0:T(8,128)(2,1)S(1)}, bf16[4,48,1024]{2,1,0:T(8,128)(2,1)S(1)}, u32[]{:S(2)}, u32[]{:S(2)}) collective-permute-start(bf16[4,48,1024]{2,1,0:T(8,128)(2,1)S(1)} %get-tuple-element.71), channel_id=1, source_target_pairs={{0,16},{1,5},{2,18},{3,7},{4,20},{5,1},{6,22},{7,3},{8,24},{9,13},... | collective-permute-start | bytes 1179656 | tf_op jit(solution)/shard_map/ppermute | solution.py:29
  68.8 3.6 %down_grad.1 = bf16[1,384,4096]{2,1,0:T(8,128)(2,1)} custom-call(bf16[4,4,48,1024]{3,2,1,0:T(8,128)(2,1)S(1)} %join_second_1.1.pieces.mine, bf16[4,4,48,1024]{3,2,1,0:T(8,128)(2,1)S(1)} %collective-permute-done.9.pieces.theirs, bf16[384,384]{1,0:T(8,128)(2,1)S(1)} %get-tuple-element.73.hidden), custom_call_target="tpu_custom_call" | custom-call | tf_op jit(solution)/shard_map/down_grad/pallas_call | solution.py:58
  72.4 6.2 %gate_up_grads.1 = (bf16[1,4096,384]{2,1,0:T(8,128)(2,1)}, bf16[1,4096,384]{2,1,0:T(8,128)(2,1)}) custom-call(bf16[4,4,48,1024]{3,2,1,0:T(8,128)(2,1)S(1)} %join_second_0.1.pieces.mine, bf16[4,4,48,1024]{3,2,1,0:T(8,128)(2,1)S(1)} %collective-permute-done.10.pieces.theirs, bf16[384,768]{1,0:T(8,128)(2,1)S(1)} %backward_hidden_1.1.d), custom_call_target="tpu_custom_call" | custom-call | tf_op jit(solution)/shard_map/gate_up_grads/pallas_call | solution.py:58
  78.6 1.8 %collective-permute-done.13.refs_6_ = bf16[4,48,1024]{2,1,0:T(8,128)(2,1)S(1)} collective-permute-done((bf16[4,48,1024]{2,1,0:T(8,128)(2,1)S(1)}, bf16[4,48,1024]{2,1,0:T(8,128)(2,1)S(1)}, u32[]{:S(2)}, u32[]{:S(2)}) %collective-permute-start.13) | collective-permute-done | bytes 393248 | tf_op jit(solution)/shard_map/ppermute | solution.py:29
  80.4 4.1 %collective-permute-done.14.refs_7_ = bf16[4,48,1024]{2,1,0:T(8,128)(2,1)S(1)} collective-permute-done((bf16[4,48,1024]{2,1,0:T(8,128)(2,1)S(1)}, bf16[4,48,1024]{2,1,0:T(8,128)(2,1)S(1)}, u32[]{:S(2)}, u32[]{:S(2)}) %collective-permute-start.14) | collective-permute-done | bytes 393248 | tf_op jit(solution)/shard_map/ppermute | solution.py:29
  84.9 1.5 %collective-permute-start.19 = (bf16[96,1024]{1,0:T(8,128)(2,1)S(1)}, bf16[96,1024]{1,0:T(8,128)(2,1)S(1)}, u32[]{:S(2)}, u32[]{:S(2)}) collective-permute-start(bf16[96,1024]{1,0:T(8,128)(2,1)S(1)} %get-tuple-element.93), channel_id=1, source_target_pairs={{0,2},{1,9},{2,0},{3,11},{4,6},{5,13},{6,4},{7,15},{8,10},{9,1},{1... | collective-permute-start | bytes 589832 | tf_op jit(solution)/shard_map/ppermute | solution.py:29
  86.4 2.7 %collective-permute-start.20 = (bf16[96,1024]{1,0:T(8,128)(2,1)S(1)}, bf16[96,1024]{1,0:T(8,128)(2,1)S(1)}, u32[]{:S(2)}, u32[]{:S(2)}) collective-permute-start(bf16[96,1024]{1,0:T(8,128)(2,1)S(1)} %get-tuple-element.94), channel_id=1, source_target_pairs={{0,4},{1,17},{2,6},{3,19},{4,0},{5,21},{6,2},{7,23},{8,12},{9,25},... | collective-permute-start | bytes 589832 | tf_op jit(solution)/shard_map/ppermute | solution.py:29
  90.6 4.3 %collective-permute-done.20.c = bf16[96,1024]{1,0:T(8,128)(2,1)S(1)} collective-permute-done((bf16[96,1024]{1,0:T(8,128)(2,1)S(1)}, bf16[96,1024]{1,0:T(8,128)(2,1)S(1)}, u32[]{:S(2)}, u32[]{:S(2)}) %collective-permute-start.20) | collective-permute-done | bytes 196640 | tf_op jit(solution)/shard_map/ppermute | solution.py:29
  94.9 2.0 %collective-permute-done.21.d = bf16[96,1024]{1,0:T(8,128)(2,1)S(1)} collective-permute-done((bf16[96,1024]{1,0:T(8,128)(2,1)S(1)}, bf16[96,1024]{1,0:T(8,128)(2,1)S(1)}, u32[]{:S(2)}, u32[]{:S(2)}) %collective-permute-start.21) | collective-permute-done | bytes 196640 | tf_op jit(solution)/shard_map/ppermute | solution.py:29
  97.2 4.1 %collective-permute-start.23 = (f32[24,1024]{1,0:T(8,128)S(1)}, f32[24,1024]{1,0:T(8,128)S(1)}, u32[]{:S(2)}, u32[]{:S(2)}) collective-permute-start(f32[24,1024]{1,0:T(8,128)S(1)} %get-tuple-element.98), channel_id=1, source_target_pairs={{0,64},{1,65},{2,66},{3,67},{4,68},{5,69},{6,70},{7,71},{8,72},{9,... | collective-permute-start | bytes 294920 | tf_op jit(solution)/shard_map/ppermute | solution.py:29
  101.8 3.1 %collective-permute-done.23.c = f32[24,1024]{1,0:T(8,128)S(1)} collective-permute-done((f32[24,1024]{1,0:T(8,128)S(1)}, f32[24,1024]{1,0:T(8,128)S(1)}, u32[]{:S(2)}, u32[]{:S(2)}) %collective-permute-start.23) | collective-permute-done | bytes 98336 | tf_op jit(solution)/shard_map/ppermute | solution.py:29
  104.9 2.2 %collective-permute-done.24.d = f32[24,1024]{1,0:T(8,128)S(1)} collective-permute-done((f32[24,1024]{1,0:T(8,128)S(1)}, f32[24,1024]{1,0:T(8,128)S(1)}, u32[]{:S(2)}, u32[]{:S(2)}) %collective-permute-start.24) | collective-permute-done | bytes 98336 | tf_op jit(solution)/shard_map/ppermute | solution.py:29
  (49 shorter events, 20.4 us)
Async XLA Ops:
  1.9 9.5 %collective-permute-start = (bf16[24,1024]{1,0:T(8,128)(2,1)S(1)}, bf16[24,1024]{1,0:T(8,128)(2,1)S(1)}, u32[]{:S(2)}, u32[]{:S(2)}) collective-permute-start(bf16[24,1024]{1,0:T(8,128)(2,1)S(1)} %get-tuple-element.56), channel_id=1, source_target_pairs={{0,32},{1,33},{2,34},{3,35},{4,36},{5,37},{6,38},{7,39},{8,40},{9,... | collective-permute-start | bytes 147464 | tf_op jit(solution)/shard_map/ppermute | solution.py:29
  3.6 7.8 %collective-permute-start.1 = (bf16[24,1024]{1,0:T(8,128)(2,1)S(1)}, bf16[24,1024]{1,0:T(8,128)(2,1)S(1)}, u32[]{:S(2)}, u32[]{:S(2)}) collective-permute-start(bf16[24,1024]{1,0:T(8,128)(2,1)S(1)} %get-tuple-element.57), channel_id=1, source_target_pairs={{0,64},{1,65},{2,66},{3,67},{4,68},{5,69},{6,70},{7,71},{8,72},{9,... | collective-permute-start | bytes 147464 | tf_op jit(solution)/shard_map/ppermute | solution.py:29
  6.5 5.3 %collective-permute-start.2 = (bf16[24,1024]{1,0:T(8,128)(2,1)S(1)}, bf16[24,1024]{1,0:T(8,128)(2,1)S(1)}, u32[]{:S(2)}, u32[]{:S(2)}) collective-permute-start(bf16[24,1024]{1,0:T(8,128)(2,1)S(1)} %get-tuple-element.58), channel_id=1, source_target_pairs={{0,96},{1,97},{2,98},{3,99},{4,100},{5,101},{6,102},{7,103},{8,104... | collective-permute-start | bytes 147464 | tf_op jit(solution)/shard_map/ppermute | solution.py:29
  12.1 8.1 %collective-permute-start.5 = (bf16[96,1024]{1,0:T(8,128)(2,1)S(1)}, bf16[96,1024]{1,0:T(8,128)(2,1)S(1)}, u32[]{:S(2)}, u32[]{:S(2)}) collective-permute-start(bf16[96,1024]{1,0:T(8,128)(2,1)S(1)} %join_y.1.a), channel_id=1, source_target_pairs={{0,6},{1,25},{2,4},{3,27},{4,2},{5,29},{6,0},{7,31},{8,14},{9,17},... | collective-permute-start | bytes 589832 | tf_op jit(solution)/shard_map/ppermute | solution.py:29
  14.9 7.2 %collective-permute-start.4 = (bf16[96,1024]{1,0:T(8,128)(2,1)S(1)}, bf16[96,1024]{1,0:T(8,128)(2,1)S(1)}, u32[]{:S(2)}, u32[]{:S(2)}) collective-permute-start(bf16[96,1024]{1,0:T(8,128)(2,1)S(1)} %join_y.1.a), channel_id=1, source_target_pairs={{0,4},{1,17},{2,6},{3,19},{4,0},{5,21},{6,2},{7,23},{8,12},{9,25},... | collective-permute-start | bytes 589832 | tf_op jit(solution)/shard_map/ppermute | solution.py:29
  15.7 6.4 %collective-permute-start.3 = (bf16[96,1024]{1,0:T(8,128)(2,1)S(1)}, bf16[96,1024]{1,0:T(8,128)(2,1)S(1)}, u32[]{:S(2)}, u32[]{:S(2)}) collective-permute-start(bf16[96,1024]{1,0:T(8,128)(2,1)S(1)} %join_y.1.a), channel_id=1, source_target_pairs={{0,2},{1,9},{2,0},{3,11},{4,6},{5,13},{6,4},{7,15},{8,10},{9,1},{1... | collective-permute-start | bytes 589832 | tf_op jit(solution)/shard_map/ppermute | solution.py:29
  22.1 22.5 %collective-permute-start.8 = (bf16[4,96,1024]{2,1,0:T(8,128)(2,1)S(1)}, bf16[4,96,1024]{2,1,0:T(8,128)(2,1)S(1)}, u32[]{:S(2)}, u32[]{:S(2)}) collective-permute-start(bf16[4,96,1024]{2,1,0:T(8,128)(2,1)S(1)} %join_first.1.a), channel_id=1, source_target_pairs={{0,24},{1,7},{2,26},{3,5},{4,28},{5,3},{6,30},{7,1},{8,16},{9,15},... | collective-permute-start | bytes 2359304 | tf_op jit(solution)/shard_map/ppermute | solution.py:29
  26.3 18.4 %collective-permute-start.7 = (bf16[4,96,1024]{2,1,0:T(8,128)(2,1)S(1)}, bf16[4,96,1024]{2,1,0:T(8,128)(2,1)S(1)}, u32[]{:S(2)}, u32[]{:S(2)}) collective-permute-start(bf16[4,96,1024]{2,1,0:T(8,128)(2,1)S(1)} %join_first.1.a), channel_id=1, source_target_pairs={{0,16},{1,5},{2,18},{3,7},{4,20},{5,1},{6,22},{7,3},{8,24},{9,13},... | collective-permute-start | bytes 2359304 | tf_op jit(solution)/shard_map/ppermute | solution.py:29
  26.3 19.4 %collective-permute-start.6 = (bf16[4,96,1024]{2,1,0:T(8,128)(2,1)S(1)}, bf16[4,96,1024]{2,1,0:T(8,128)(2,1)S(1)}, u32[]{:S(2)}, u32[]{:S(2)}) collective-permute-start(bf16[4,96,1024]{2,1,0:T(8,128)(2,1)S(1)} %join_first.1.a), channel_id=1, source_target_pairs={{0,8},{1,3},{2,10},{3,1},{4,12},{5,7},{6,14},{7,5},{8,0},{9,11},{1... | collective-permute-start | bytes 2359304 | tf_op jit(solution)/shard_map/ppermute | solution.py:29
  45.9 6.9 %collective-permute-start.9 = (bf16[4,4,48,1024]{3,2,1,0:T(8,128)(2,1)S(1)}, bf16[4,4,48,1024]{3,2,1,0:T(8,128)(2,1)S(1)}, u32[]{:S(2)}, u32[]{:S(2)}) collective-permute-start(bf16[4,4,48,1024]{3,2,1,0:T(8,128)(2,1)S(1)} %join_second_1.1.pieces.mine), channel_id=1, source_target_pairs={{0,1},{1,0},{2,3},{3,2},{4,5},{5,4},{6,7},{7,6},{8,9},{9,8},{10,11... | collective-permute-start | bytes 4718600 | tf_op jit(solution)/shard_map/ppermute | solution.py:29
  51.6 5.2 %collective-permute-start.15 = (bf16[4,4,48,1024]{3,2,1,0:T(8,128)(2,1)S(1)}, bf16[4,4,48,1024]{3,2,1,0:T(8,128)(2,1)S(1)}, u32[]{:S(2)}, u32[]{:S(2)}) collective-permute-start(bf16[4,4,48,1024]{3,2,1,0:T(8,128)(2,1)S(1)} %out_rows_1.1), channel_id=1, source_target_pairs={{0,1},{1,0},{2,3},{3,2},{4,5},{5,4},{6,7},{7,6},{8,9},{9,8},{10,11... | collective-permute-start | bytes 4718600 | tf_op jit(solution)/shard_map/ppermute | solution.py:29
  55.4 8.3 %collective-permute-start.11 = (bf16[4,4,48,1024]{3,2,1,0:T(8,128)(2,1)S(1)}, bf16[4,4,48,1024]{3,2,1,0:T(8,128)(2,1)S(1)}, u32[]{:S(2)}, u32[]{:S(2)}) collective-permute-start(bf16[4,4,48,1024]{3,2,1,0:T(8,128)(2,1)S(1)} %back_rows_1.1), channel_id=1, source_target_pairs={{0,1},{1,0},{2,3},{3,2},{4,5},{5,4},{6,7},{7,6},{8,9},{9,8},{10,11... | collective-permute-start | bytes 4718600 | tf_op jit(solution)/shard_map/ppermute | solution.py:29
  57.2 11.5 %collective-permute-start.16 = (bf16[4,48,1024]{2,1,0:T(8,128)(2,1)S(1)}, bf16[4,48,1024]{2,1,0:T(8,128)(2,1)S(1)}, u32[]{:S(2)}, u32[]{:S(2)}) collective-permute-start(bf16[4,48,1024]{2,1,0:T(8,128)(2,1)S(1)} %get-tuple-element.75), channel_id=1, source_target_pairs={{0,8},{1,3},{2,10},{3,1},{4,12},{5,7},{6,14},{7,5},{8,0},{9,11},{1... | collective-permute-start | bytes 1179656 | tf_op jit(solution)/shard_map/ppermute | solution.py:29
  59.8 18.8 %collective-permute-start.17 = (bf16[4,48,1024]{2,1,0:T(8,128)(2,1)S(1)}, bf16[4,48,1024]{2,1,0:T(8,128)(2,1)S(1)}, u32[]{:S(2)}, u32[]{:S(2)}) collective-permute-start(bf16[4,48,1024]{2,1,0:T(8,128)(2,1)S(1)} %get-tuple-element.76), channel_id=1, source_target_pairs={{0,16},{1,5},{2,18},{3,7},{4,20},{5,1},{6,22},{7,3},{8,24},{9,13},... | collective-permute-start | bytes 1179656 | tf_op jit(solution)/shard_map/ppermute | solution.py:29
  63.5 15.0 %collective-permute-start.18 = (bf16[4,48,1024]{2,1,0:T(8,128)(2,1)S(1)}, bf16[4,48,1024]{2,1,0:T(8,128)(2,1)S(1)}, u32[]{:S(2)}, u32[]{:S(2)}) collective-permute-start(bf16[4,48,1024]{2,1,0:T(8,128)(2,1)S(1)} %get-tuple-element.77), channel_id=1, source_target_pairs={{0,24},{1,7},{2,26},{3,5},{4,28},{5,3},{6,30},{7,1},{8,16},{9,15},... | collective-permute-start | bytes 1179656 | tf_op jit(solution)/shard_map/ppermute | solution.py:29
  64.0 14.6 %collective-permute-start.12 = (bf16[4,48,1024]{2,1,0:T(8,128)(2,1)S(1)}, bf16[4,48,1024]{2,1,0:T(8,128)(2,1)S(1)}, u32[]{:S(2)}, u32[]{:S(2)}) collective-permute-start(bf16[4,48,1024]{2,1,0:T(8,128)(2,1)S(1)} %get-tuple-element.70), channel_id=1, source_target_pairs={{0,8},{1,3},{2,10},{3,1},{4,12},{5,7},{6,14},{7,5},{8,0},{9,11},{1... | collective-permute-start | bytes 1179656 | tf_op jit(solution)/shard_map/ppermute | solution.py:29
  64.1 16.3 %collective-permute-start.13 = (bf16[4,48,1024]{2,1,0:T(8,128)(2,1)S(1)}, bf16[4,48,1024]{2,1,0:T(8,128)(2,1)S(1)}, u32[]{:S(2)}, u32[]{:S(2)}) collective-permute-start(bf16[4,48,1024]{2,1,0:T(8,128)(2,1)S(1)} %get-tuple-element.71), channel_id=1, source_target_pairs={{0,16},{1,5},{2,18},{3,7},{4,20},{5,1},{6,22},{7,3},{8,24},{9,13},... | collective-permute-start | bytes 1179656 | tf_op jit(solution)/shard_map/ppermute | solution.py:29
  68.7 15.8 %collective-permute-start.14 = (bf16[4,48,1024]{2,1,0:T(8,128)(2,1)S(1)}, bf16[4,48,1024]{2,1,0:T(8,128)(2,1)S(1)}, u32[]{:S(2)}, u32[]{:S(2)}) collective-permute-start(bf16[4,48,1024]{2,1,0:T(8,128)(2,1)S(1)} %get-tuple-element.72), channel_id=1, source_target_pairs={{0,24},{1,7},{2,26},{3,5},{4,28},{5,3},{6,30},{7,1},{8,16},{9,15},... | collective-permute-start | bytes 1179656 | tf_op jit(solution)/shard_map/ppermute | solution.py:29
  84.9 5.7 %collective-permute-start.19 = (bf16[96,1024]{1,0:T(8,128)(2,1)S(1)}, bf16[96,1024]{1,0:T(8,128)(2,1)S(1)}, u32[]{:S(2)}, u32[]{:S(2)}) collective-permute-start(bf16[96,1024]{1,0:T(8,128)(2,1)S(1)} %get-tuple-element.93), channel_id=1, source_target_pairs={{0,2},{1,9},{2,0},{3,11},{4,6},{5,13},{6,4},{7,15},{8,10},{9,1},{1... | collective-permute-start | bytes 589832 | tf_op jit(solution)/shard_map/ppermute | solution.py:29
  86.4 8.6 %collective-permute-start.20 = (bf16[96,1024]{1,0:T(8,128)(2,1)S(1)}, bf16[96,1024]{1,0:T(8,128)(2,1)S(1)}, u32[]{:S(2)}, u32[]{:S(2)}) collective-permute-start(bf16[96,1024]{1,0:T(8,128)(2,1)S(1)} %get-tuple-element.94), channel_id=1, source_target_pairs={{0,4},{1,17},{2,6},{3,19},{4,0},{5,21},{6,2},{7,23},{8,12},{9,25},... | collective-permute-start | bytes 589832 | tf_op jit(solution)/shard_map/ppermute | solution.py:29
  89.1 7.9 %collective-permute-start.21 = (bf16[96,1024]{1,0:T(8,128)(2,1)S(1)}, bf16[96,1024]{1,0:T(8,128)(2,1)S(1)}, u32[]{:S(2)}, u32[]{:S(2)}) collective-permute-start(bf16[96,1024]{1,0:T(8,128)(2,1)S(1)} %get-tuple-element.95), channel_id=1, source_target_pairs={{0,6},{1,25},{2,4},{3,27},{4,2},{5,29},{6,0},{7,31},{8,14},{9,17},... | collective-permute-start | bytes 589832 | tf_op jit(solution)/shard_map/ppermute | solution.py:29
  97.0 4.8 %collective-permute-start.22 = (f32[24,1024]{1,0:T(8,128)S(1)}, f32[24,1024]{1,0:T(8,128)S(1)}, u32[]{:S(2)}, u32[]{:S(2)}) collective-permute-start(f32[24,1024]{1,0:T(8,128)S(1)} %get-tuple-element.97), channel_id=1, source_target_pairs={{0,32},{1,33},{2,34},{3,35},{4,36},{5,37},{6,38},{7,39},{8,40},{9,... | collective-permute-start | bytes 294920 | tf_op jit(solution)/shard_map/ppermute | solution.py:29
  97.2 7.8 %collective-permute-start.23 = (f32[24,1024]{1,0:T(8,128)S(1)}, f32[24,1024]{1,0:T(8,128)S(1)}, u32[]{:S(2)}, u32[]{:S(2)}) collective-permute-start(f32[24,1024]{1,0:T(8,128)S(1)} %get-tuple-element.98), channel_id=1, source_target_pairs={{0,64},{1,65},{2,66},{3,67},{4,68},{5,69},{6,70},{7,71},{8,72},{9,... | collective-permute-start | bytes 294920 | tf_op jit(solution)/shard_map/ppermute | solution.py:29
  101.3 5.8 %collective-permute-start.24 = (f32[24,1024]{1,0:T(8,128)S(1)}, f32[24,1024]{1,0:T(8,128)S(1)}, u32[]{:S(2)}, u32[]{:S(2)}) collective-permute-start(f32[24,1024]{1,0:T(8,128)S(1)} %get-tuple-element.99), channel_id=1, source_target_pairs={{0,96},{1,97},{2,98},{3,99},{4,100},{5,101},{6,102},{7,103},{8,104... | collective-permute-start | bytes 294920 | tf_op jit(solution)/shard_map/ppermute | solution.py:29
  (1 other events, 3.5 us)

commit v2 on v1

--- a/solution.py
+++ b/solution.py
@@ -45,8 +45,11 @@
     return send(value, lambda i: i ^ (mask << (1 if i & 1 else 3)))
 
 
+ORDER = (0, 3, 2, 1)
+
+
 def exchange(values, over):
-    return [values[0]] + [over(values[m], m) for m in (1, 2, 3)]
+    return [values[0]] + [over(values[m], m) for m in ORDER[1:]]
 
 
 def call(kernel, name, specs, shapes, operands, mib=8, scratch=(), out=None):
@@ -143,7 +146,7 @@
 def join_y(parts):
     total = 4 * PAIR
 
-    def kernel(a, b, c, d, out):
+    def kernel(a, d, c, b, out):
         stacked = jnp.concatenate([p[...].astype(F32) for p in (a, b, c, d)], axis=0).astype(BF16)
         to = lax.broadcasted_iota(jnp.int32, (total, total), 0)
         come = lax.broadcasted_iota(jnp.int32, (total, total), 1)
@@ -169,19 +172,20 @@
 
 
 def join_first(parts):
-    def kernel(a, b, c, d, out):
+    def kernel(a, d, c, b, x_out, cot_out):
+        for m, part in enumerate((a, b, c, d)):
+            x_out[m] = part[:BLOCK, :]
+            cot_out[m] = part[BLOCK:, :]
+
+    return call(kernel, "join_first", [VMEM] * 4, [((4, BLOCK, WIDTH), BF16)] * 2, parts)
+
+
+def join_second(parts):
+    def kernel(a, d, c, b, out):
         for m, part in enumerate((a, b, c, d)):
             out[m] = part[...]
 
-    return call(kernel, "join_first", [VMEM] * 4, [((4, 2 * BLOCK, WIDTH), BF16)], parts)[0]
-
-
-def join_second(parts, half):
-    def kernel(a, b, c, d, out):
-        for m, part in enumerate((a, b, c, d)):
-            out[m] = part[:, half * BLOCK : (half + 1) * BLOCK, :]
-
-    return call(kernel, f"join_second_{half}", [VMEM] * 4, [((4, 4, BLOCK, WIDTH), BF16)], parts)[0]
+    return call(kernel, "join_second", [VMEM] * 4, [((4, 4, BLOCK, WIDTH), BF16)], parts)[0]
 
 
 def place(core, xlm, zm, xhm):
@@ -271,46 +275,36 @@
     return call(kernel, f"back_rows_{cm}", [VMEM, VMEM], shapes, (d_both, w_both))[0]
 
 
-def gate_up_grads(x_pieces, d_both):
-    def kernel(mine, theirs, d, gate_out, up_out, total, sems):
+def weight_grads(x_pieces, cot_pieces, d_both, hidden):
+    def kernel(x_mine, x_theirs, cot_mine, cot_theirs, d, hidden, gate_out, up_out, down_out, both, down, sems):
         shard = lax.axis_index("shard")
-        copies = [None] * 4
+        copies = []
         for fm in range(4):
-            slot = fm % 2
+            side = (shard & 1) ^ (fm % 2)
             if fm >= 2:
                 wait_all(copies[fm - 2])
-            rows = rows_of((shard & 1) ^ (fm % 2), fm // 2, theirs if fm % 2 else mine)
-            total[slot] = lax.dot_general(rows, d[...], TN, preferred_element_type=F32).astype(BF16)
-            sources = [total.at[slot, :, :UNITS], total.at[slot, :, UNITS:]]
+            slot = fm % 2
+            rows = rows_of(side, fm // 2, x_theirs if fm % 2 else x_mine)
+            both[slot] = lax.dot_general(rows, d[...], TN, preferred_element_type=F32).astype(BF16)
+            sources = [both.at[slot, :, :UNITS], both.at[slot, :, UNITS:]]
             targets = [gate_out.at[0, at(shard, fm), :], up_out.at[0, at(shard, fm), :]]
-            copies[fm] = fetch(sources, targets, sems.at[slot])
+            started = fetch(sources, targets, sems.at[slot])
+            rows = rows_of(side, fm // 2, cot_theirs if fm % 2 else cot_mine)
+            down[slot] = lax.dot_general(hidden[...], rows, TN, preferred_element_type=F32).astype(BF16)
+            last = pltpu.make_async_copy(down.at[slot], down_out.at[0, :, at(shard, fm)], sems.at[slot, 2])
+            last.start()
+            copies.append(started + [last])
         wait_all(copies[2])
         wait_all(copies[3])
 
-    shapes = [((1, 4 * WIDTH, UNITS), BF16)] * 2
-    scratch = [pltpu.VMEM((2, WIDTH, 2 * UNITS), BF16), pltpu.SemaphoreType.DMA((2, 2))]
-    operands = (*x_pieces, d_both)
-    return call(kernel, "gate_up_grads", [VMEM] * 3, shapes, operands, 12, scratch, HBM)
-
-
-def down_grad(cot_pieces, hidden):
-    def kernel(mine, theirs, hidden, out, total, sems):
-        shard = lax.axis_index("shard")
-        copies = [None] * 4
-        for fm in range(4):
-            slot = fm % 2
-            if fm >= 2:
-                wait_all(copies[fm - 2])
-            rows = rows_of((shard & 1) ^ (fm % 2), fm // 2, theirs if fm % 2 else mine)
-            total[slot] = lax.dot_general(hidden[...], rows, TN, preferred_element_type=F32).astype(BF16)
-            copies[fm] = fetch([total.at[slot]], [out.at[0, :, at(shard, fm)]], sems.at[slot])
-        wait_all(copies[2])
-        wait_all(copies[3])
-
-    shapes = [((1, UNITS, 4 * WIDTH), BF16)]
-    scratch = [pltpu.VMEM((2, UNITS, WIDTH), BF16), pltpu.SemaphoreType.DMA((2, 1))]
-    operands = (*cot_pieces, hidden)
-    return call(kernel, "down_grad", [VMEM] * 3, shapes, operands, 10, scratch, HBM)[0]
+    shapes = [((1, 4 * WIDTH, UNITS), BF16)] * 2 + [((1, UNITS, 4 * WIDTH), BF16)]
+    scratch = [
+        pltpu.VMEM((2, WIDTH, 2 * UNITS), BF16),
+        pltpu.VMEM((2, UNITS, WIDTH), BF16),
+        pltpu.SemaphoreType.DMA((2, 3)),
+    ]
+    operands = (*x_pieces, *cot_pieces, d_both, hidden)
+    return call(kernel, "weight_grads", [VMEM] * 6, shapes, operands, 14, scratch, HBM)
 
 
 def wait_all(copies):
@@ -327,7 +321,7 @@
 
 
 def sum_second(pieces):
-    def kernel(a, b, c, d, *outs):
+    def kernel(a, d, c, b, *outs):
         for m in range(4):
             total = (a[m].astype(F32) + b[m].astype(F32)) + (c[m].astype(F32) + d[m].astype(F32))
             outs[m][...] = total.astype(outs[m].dtype)
@@ -349,19 +343,19 @@
 
 
 def sum_first(blocks):
-    def kernel(a, b, c, d, *outs):
+    def kernel(a, d, c, b, *outs):
         total = (a[...] + b[...].astype(F32)) + (c[...].astype(F32) + d[...].astype(F32))
         for m in range(4):
-            for half in range(2):
-                row = half * BLOCK + m * SLOTS
-                outs[m][half * SLOTS : (half + 1) * SLOTS, :] = total[row : row + SLOTS]
-
-    return call(kernel, "sum_first", [VMEM] * 4, [((PAIR, WIDTH), F32)] * 4, blocks)
+            halves = [total[half * BLOCK + m * SLOTS :][:SLOTS] for half in range(2)]
+            outs[m][...] = jnp.concatenate(halves, axis=0).astype(outs[m].dtype)
+
+    shapes = [((PAIR, WIDTH), F32)] + [((PAIR, WIDTH), BF16)] * 3
+    return call(kernel, "sum_first", [VMEM] * 4, shapes, blocks)
 
 
 def combine(matrix, parts):
-    def kernel(matrix, a, b, c, d, outputs, grads):
-        stacked = jnp.concatenate([p[...] for p in (a, b, c, d)], axis=0)
+    def kernel(matrix, a, d, c, b, outputs, grads):
+        stacked = jnp.concatenate([p[...].astype(F32) for p in (a, b, c, d)], axis=0)
         total = lax.dot_general(
             matrix[...], stacked, TN, precision=lax.Precision.HIGHEST, preferred_element_type=F32
         )
@@ -375,30 +369,27 @@
     routing = (prev_counts, hosts, routes.T, gate_probs.T)
     tie = lax.optimization_barrier
     payload = exchange(pack(routing, tokens, grad_out), over_y)
-    payload, matrix, (w_both, w_down) = tie(
-        (payload, combine_matrix(routing), load_weights(w_gate, w_up, w_down))
+    payload, matrix = tie((payload, combine_matrix(routing)))
+    both, (w_both, w_down) = tie(
+        (exchange([join_y(payload)] * 4, over_first), load_weights(w_gate, w_up, w_down))
     )
-    both = join_first(exchange([join_y(payload)] * 4, over_first))
-    both = exchange([both] * 4, over_second)
-    x_mine = join_second(both, 0)
-    x_theirs = over_core(x_mine)
-    cot_mine = join_second(both, 1)
+    x_quarter, cot_quarter = join_first(both)
+    x_quarters = exchange([x_quarter] * 4, over_second)
+    x_mine = join_second(x_quarters)
+    x_theirs = [over_core(x) for x in x_quarters]
+    cot_mine = join_second(exchange([cot_quarter] * 4, over_second))
+    (part,) = forward(0, x_mine, w_both, None)
+    x_theirs, cot_mine, part = tie((x_theirs, cot_mine, part))
+    x_theirs = join_second(x_theirs)
     cot_theirs = over_core(cot_mine)
-
-    (part,) = forward(0, x_mine, w_both, None)
-    back_part = backward_hidden(0, cot_mine, w_down, None, None)
     gate_up, hidden = forward(1, x_theirs, w_both, part)
-    d_both = backward_hidden(1, cot_theirs, w_down, back_part, gate_up)
+    out_theirs = over_core(out_rows(1, hidden, w_down))
+    part = backward_hidden(0, cot_mine, w_down, None, None)
+    d_both = backward_hidden(1, cot_theirs, w_down, part, gate_up)
     back_theirs = over_core(back_rows(1, d_both, w_both))
-    back_mine = back_rows(0, d_both, w_both)
-    back_pieces = exchange(sum_cores(back_mine, back_theirs), over_second)
-    out_theirs = over_core(out_rows(1, hidden, w_down))
-    out_mine = out_rows(0, hidden, w_down)
-    out_pieces = exchange(sum_cores(out_mine, out_theirs), over_second)
-    grads = (
-        *gate_up_grads((x_mine, x_theirs), d_both),
-        down_grad((cot_mine, cot_theirs), hidden),
-    )
+    out_pieces = exchange(sum_cores(out_rows(0, hidden, w_down), out_theirs), over_second)
+    back_pieces = exchange(sum_cores(back_rows(0, d_both, w_both), back_theirs), over_second)
+    grads = weight_grads((x_mine, x_theirs), (cot_mine, cot_theirs), d_both, hidden)
     back_pieces, out_pieces, grads = tie((back_pieces, out_pieces, grads))
     blocks = exchange(sum_second_both(sum_second(out_pieces), back_pieces), over_first)
     parts = exchange(sum_first(blocks), over_y)

time: 108 us -> 97 us (0.90)
  waiting for transfers between devices: 44.5 us -> 35.8 us
  Pallas kernels: 28 us -> 25.4 us
    ppermute x25 -> x31, waiting for transfers between devices: 44.5 us -> 35.8 us  [send(): return lax.ppermute(value, AXES, [(i, flip(i)) for i in range(128)])]
    pallas_call x23, Pallas kernels: 28 us -> 25.4 us  [call(): pl.pallas_call(kernel, out_shape=[jax.ShapeDtypeStruct(s, d) if out else...]
    ppermute x25 -> x31, starting transfers between devices: 34.7 us -> 34.7 us  [send(): return lax.ppermute(value, AXES, [(i, flip(i)) for i in range(128)])]
  transfers between devices with their start and end apart: 25 -> 31, of which waited for: 13 -> 16; matrix products, arithmetic and copies ran while one was open for 0% -> 0% of each run, Pallas kernels for 23% -> 23%
where the time goes in v2:
time: 97 us; the launch traced here: 96.8 us
  waiting for transfers between devices  35.8 us (37%)
  starting transfers between devices  34.7 us (36%)
  Pallas kernels  25.4 us (26%)
    ppermute x31, waiting for transfers between devices, send(): return lax.ppermute(value, AXES, [(i, flip(i)) for i in range(128)])  35.8 us
    ppermute x31, starting transfers between devices, send(): return lax.ppermute(value, AXES, [(i, flip(i)) for i in range(128)])  34.7 us
    pallas_call x23, Pallas kernels, call(): pl.pallas_call(kernel, out_shape=[jax.ShapeDtypeStruct(s, d) if out else...  25.4 us
  transfers between devices with their start and end apart: 31, of which 16 were waited for; matrix products, arithmetic and copies ran while one was open for 0% of the time, Pallas kernels for 23%

profile of v2, /device:TPU:0, one launch (start us, length us, event | category | flops | bytes accessed | tf_op | source)
XLA Modules:
  0.0 96.8 jit_solution(3200202202936661957)
XLA Ops:
  1.9 3.2 %collective-permute-start = (bf16[24,1024]{1,0:T(8,128)(2,1)S(1)}, bf16[24,1024]{1,0:T(8,128)(2,1)S(1)}, u32[]{:S(2)}, u32[]{:S(2)}) collective-permute-start(bf16[24,1024]{1,0:T(8,128)(2,1)S(1)} %get-tuple-element.69), channel_id=1, source_target_pairs={{0,96},{1,97},{2,98},{3,99},{4,100},{5,101},{6,102},{7,103},{8,104... | collective-permute-start | bytes 147464 | tf_op jit(solution)/shard_map/ppermute | solution.py:29
  7.3 3.4 %collective-permute-done.1.c = bf16[24,1024]{1,0:T(8,128)(2,1)S(1)} collective-permute-done((bf16[24,1024]{1,0:T(8,128)(2,1)S(1)}, bf16[24,1024]{1,0:T(8,128)(2,1)S(1)}, u32[]{:S(2)}, u32[]{:S(2)}) %collective-permute-start.1) | collective-permute-done | bytes 49184 | tf_op jit(solution)/shard_map/ppermute | solution.py:29
  10.9 2.8 %collective-permute-start.3 = (bf16[96,1024]{1,0:T(8,128)(2,1)S(1)}, bf16[96,1024]{1,0:T(8,128)(2,1)S(1)}, u32[]{:S(2)}, u32[]{:S(2)}) collective-permute-start(bf16[96,1024]{1,0:T(8,128)(2,1)S(1)} %join_y.1.a), channel_id=1, source_target_pairs={{0,6},{1,25},{2,4},{3,27},{4,2},{5,29},{6,0},{7,31},{8,14},{9,17},... | collective-permute-start | bytes 589832 | tf_op jit(solution)/shard_map/ppermute | solution.py:29
  15.1 3.8 %load_weights.1 = (bf16[4096,768]{1,0:T(8,128)(2,1)S(1)}, bf16[384,4096]{1,0:T(8,128)(2,1)S(1)}) custom-call(bf16[1,4096,384]{2,1,0:T(8,128)(2,1)} %wg.1, bf16[1,4096,384]{2,1,0:T(8,128)(2,1)} %wu.1, bf16[1,384,4096]{2,1,0:T(8,128)(2,1)} %wd.1), custom_call_target="tpu_custom_call" | custom-call | tf_op jit(solution)/shard_map/load_weights/pallas_call | solution.py:61
  19.1 1.8 %collective-permute-done.4.c = bf16[96,1024]{1,0:T(8,128)(2,1)S(1)} collective-permute-done((bf16[96,1024]{1,0:T(8,128)(2,1)S(1)}, bf16[96,1024]{1,0:T(8,128)(2,1)S(1)}, u32[]{:S(2)}, u32[]{:S(2)}) %collective-permute-start.4) | collective-permute-done | bytes 196640 | tf_op jit(solution)/shard_map/ppermute | solution.py:29
  21.0 4.1 %collective-permute-start.7 = (bf16[4,48,1024]{2,1,0:T(8,128)(2,1)S(1)}, bf16[4,48,1024]{2,1,0:T(8,128)(2,1)S(1)}, u32[]{:S(2)}, u32[]{:S(2)}) collective-permute-start(bf16[4,48,1024]{2,1,0:T(8,128)(2,1)S(1)} %get-tuple-element.83.a), channel_id=1, source_target_pairs={{0,24},{1,7},{2,26},{3,5},{4,28},{5,3},{6,30},{7,1},{8,16},{9,15},... | collective-permute-start | bytes 1179656 | tf_op jit(solution)/shard_map/ppermute | solution.py:29
  26.0 3.1 %collective-permute-start.13 = (bf16[4,48,1024]{2,1,0:T(8,128)(2,1)S(1)}, bf16[4,48,1024]{2,1,0:T(8,128)(2,1)S(1)}, u32[]{:S(2)}, u32[]{:S(2)}) collective-permute-start(bf16[4,48,1024]{2,1,0:T(8,128)(2,1)S(1)} %get-tuple-element.84.a), channel_id=1, source_target_pairs={{0,24},{1,7},{2,26},{3,5},{4,28},{5,3},{6,30},{7,1},{8,16},{9,15},... | collective-permute-start | bytes 1179656 | tf_op jit(solution)/shard_map/ppermute | solution.py:29
  29.2 5.9 %collective-permute-done.7.d = bf16[4,48,1024]{2,1,0:T(8,128)(2,1)S(1)} collective-permute-done((bf16[4,48,1024]{2,1,0:T(8,128)(2,1)S(1)}, bf16[4,48,1024]{2,1,0:T(8,128)(2,1)S(1)}, u32[]{:S(2)}, u32[]{:S(2)}) %collective-permute-start.7) | collective-permute-done | bytes 393248 | tf_op jit(solution)/shard_map/ppermute | solution.py:29
  36.7 6.8 %collective-permute-done.13.d = bf16[4,48,1024]{2,1,0:T(8,128)(2,1)S(1)} collective-permute-done((bf16[4,48,1024]{2,1,0:T(8,128)(2,1)S(1)}, bf16[4,48,1024]{2,1,0:T(8,128)(2,1)S(1)}, u32[]{:S(2)}, u32[]{:S(2)}) %collective-permute-start.13) | collective-permute-done | bytes 393248 | tf_op jit(solution)/shard_map/ppermute | solution.py:29
  44.1 1.4 %forward_0.1.refs_0_ = f32[384,768]{1,0:T(8,128)S(1)} custom-call(bf16[4,4,48,1024]{3,2,1,0:T(8,128)(2,1)S(1)} %join_second.4.pieces.x_mine, bf16[4096,768]{1,0:T(8,128)(2,1)S(1)} %get-tuple-element.85.w), custom_call_target="tpu_custom_call" | custom-call | tf_op jit(solution)/shard_map/forward_0/pallas_call | solution.py:61
  46.0 1.4 %forward_1.1 = (f32[384,768]{1,0:T(8,128)S(1)}, bf16[384,384]{1,0:T(8,128)(2,1)S(1)}) custom-call(bf16[4,4,48,1024]{3,2,1,0:T(8,128)(2,1)S(1)} %join_second.5.pieces.x_theirs, bf16[4096,768]{1,0:T(8,128)(2,1)S(1)} %get-tuple-element.85.w, f32[384,768]{1,0:T(8,128)S(1)} %forward_0.1.refs_0_), custom_call_target="tpu_custom_call" | custom-call | tf_op jit(solution)/shard_map/forward_1/pallas_call | solution.py:61
  51.0 1.4 %back_rows_1.1 = bf16[4,4,48,1024]{3,2,1,0:T(8,128)(2,1)S(1)} custom-call(bf16[384,768]{1,0:T(8,128)(2,1)S(1)} %backward_hidden_1.1.d, bf16[4096,768]{1,0:T(8,128)(2,1)S(1)} %get-tuple-element.85.w), custom_call_target="tpu_custom_call" | custom-call | tf_op jit(solution)/shard_map/back_rows_1/pallas_call | solution.py:61
  54.1 3.3 %collective-permute-start.22 = (bf16[4,48,1024]{2,1,0:T(8,128)(2,1)S(1)}, bf16[4,48,1024]{2,1,0:T(8,128)(2,1)S(1)}, u32[]{:S(2)}, u32[]{:S(2)}) collective-permute-start(bf16[4,48,1024]{2,1,0:T(8,128)(2,1)S(1)} %get-tuple-element.100), channel_id=1, source_target_pairs={{0,24},{1,7},{2,26},{3,5},{4,28},{5,3},{6,30},{7,1},{8,16},{9,15},... | collective-permute-start | bytes 1179656 | tf_op jit(solution)/shard_map/ppermute | solution.py:29
  57.5 1.4 %back_rows_0.1.a = bf16[4,4,48,1024]{3,2,1,0:T(8,128)(2,1)S(1)} custom-call(bf16[384,768]{1,0:T(8,128)(2,1)S(1)} %backward_hidden_1.1.d, bf16[4096,768]{1,0:T(8,128)(2,1)S(1)} %get-tuple-element.85.w), custom_call_target="tpu_custom_call" | custom-call | tf_op jit(solution)/shard_map/back_rows_0/pallas_call | solution.py:61
  60.2 3.3 %collective-permute-start.18 = (bf16[4,48,1024]{2,1,0:T(8,128)(2,1)S(1)}, bf16[4,48,1024]{2,1,0:T(8,128)(2,1)S(1)}, u32[]{:S(2)}, u32[]{:S(2)}) collective-permute-start(bf16[4,48,1024]{2,1,0:T(8,128)(2,1)S(1)} %get-tuple-element.95), channel_id=1, source_target_pairs={{0,24},{1,7},{2,26},{3,5},{4,28},{5,3},{6,30},{7,1},{8,16},{9,15},... | collective-permute-start | bytes 1179656 | tf_op jit(solution)/shard_map/ppermute | solution.py:29
  63.6 3.4 %collective-permute-done.22.d = bf16[4,48,1024]{2,1,0:T(8,128)(2,1)S(1)} collective-permute-done((bf16[4,48,1024]{2,1,0:T(8,128)(2,1)S(1)}, bf16[4,48,1024]{2,1,0:T(8,128)(2,1)S(1)}, u32[]{:S(2)}, u32[]{:S(2)}) %collective-permute-start.22) | collective-permute-done | bytes 393248 | tf_op jit(solution)/shard_map/ppermute | solution.py:29
  67.0 7.0 %weight_grads.1 = (bf16[1,4096,384]{2,1,0:T(8,128)(2,1)}, bf16[1,4096,384]{2,1,0:T(8,128)(2,1)}, bf16[1,384,4096]{2,1,0:T(8,128)(2,1)}) custom-call(bf16[4,4,48,1024]{3,2,1,0:T(8,128)(2,1)S(1)} %join_second.4.pieces.x_mine, bf16[4,4,48,1024]{3,2,1,0:T(8,128)(2,1)S(1)} %join_second.5.pieces.x_theirs, bf16[4,4,48,1024]{3,2,1,0:T(8,128)(2,1)S(1)} %join_second.3.pieces.cot_mine, ...), custom_call_target="tpu_custom_call" | custom-call | tf_op jit(solution)/shard_map/weight_grads/pallas_call | solution.py:61
  74.0 1.4 %collective-permute-done.18.refs_5_ = bf16[4,48,1024]{2,1,0:T(8,128)(2,1)S(1)} collective-permute-done((bf16[4,48,1024]{2,1,0:T(8,128)(2,1)S(1)}, bf16[4,48,1024]{2,1,0:T(8,128)(2,1)S(1)}, u32[]{:S(2)}, u32[]{:S(2)}) %collective-permute-start.18) | collective-permute-done | bytes 393248 | tf_op jit(solution)/shard_map/ppermute | solution.py:29
  76.7 1.6 %collective-permute-done.20.refs_7_ = bf16[4,48,1024]{2,1,0:T(8,128)(2,1)S(1)} collective-permute-done((bf16[4,48,1024]{2,1,0:T(8,128)(2,1)S(1)}, bf16[4,48,1024]{2,1,0:T(8,128)(2,1)S(1)}, u32[]{:S(2)}, u32[]{:S(2)}) %collective-permute-start.20) | collective-permute-done | bytes 393248 | tf_op jit(solution)/shard_map/ppermute | solution.py:29
  78.7 2.7 %collective-permute-start.25 = (bf16[96,1024]{1,0:T(8,128)(2,1)S(1)}, bf16[96,1024]{1,0:T(8,128)(2,1)S(1)}, u32[]{:S(2)}, u32[]{:S(2)}) collective-permute-start(bf16[96,1024]{1,0:T(8,128)(2,1)S(1)} %get-tuple-element.119), channel_id=1, source_target_pairs={{0,6},{1,25},{2,4},{3,27},{4,2},{5,29},{6,0},{7,31},{8,14},{9,17},... | collective-permute-start | bytes 589832 | tf_op jit(solution)/shard_map/ppermute | solution.py:29
  82.9 3.9 %collective-permute-done.25.d = bf16[96,1024]{1,0:T(8,128)(2,1)S(1)} collective-permute-done((bf16[96,1024]{1,0:T(8,128)(2,1)S(1)}, bf16[96,1024]{1,0:T(8,128)(2,1)S(1)}, u32[]{:S(2)}, u32[]{:S(2)}) %collective-permute-start.25) | collective-permute-done | bytes 196640 | tf_op jit(solution)/shard_map/ppermute | solution.py:29
  86.8 1.8 %collective-permute-done.26.c = bf16[96,1024]{1,0:T(8,128)(2,1)S(1)} collective-permute-done((bf16[96,1024]{1,0:T(8,128)(2,1)S(1)}, bf16[96,1024]{1,0:T(8,128)(2,1)S(1)}, u32[]{:S(2)}, u32[]{:S(2)}) %collective-permute-start.26) | collective-permute-done | bytes 196640 | tf_op jit(solution)/shard_map/ppermute | solution.py:29
  91.2 1.8 %collective-permute-start.30 = (bf16[24,1024]{1,0:T(8,128)(2,1)S(1)}, bf16[24,1024]{1,0:T(8,128)(2,1)S(1)}, u32[]{:S(2)}, u32[]{:S(2)}) collective-permute-start(bf16[24,1024]{1,0:T(8,128)(2,1)S(1)} %get-tuple-element.125), channel_id=1, source_target_pairs={{0,32},{1,33},{2,34},{3,35},{4,36},{5,37},{6,38},{7,39},{8,40},{9,... | collective-permute-start | bytes 147464 | tf_op jit(solution)/shard_map/ppermute | solution.py:29
  94.2 1.6 %collective-permute-done.29.c = bf16[24,1024]{1,0:T(8,128)(2,1)S(1)} collective-permute-done((bf16[24,1024]{1,0:T(8,128)(2,1)S(1)}, bf16[24,1024]{1,0:T(8,128)(2,1)S(1)}, u32[]{:S(2)}, u32[]{:S(2)}) %collective-permute-start.29) | collective-permute-done | bytes 49184 | tf_op jit(solution)/shard_map/ppermute | solution.py:29
  (61 shorter events, 23.5 us)
Async XLA Ops:
  1.9 5.4 %collective-permute-start = (bf16[24,1024]{1,0:T(8,128)(2,1)S(1)}, bf16[24,1024]{1,0:T(8,128)(2,1)S(1)}, u32[]{:S(2)}, u32[]{:S(2)}) collective-permute-start(bf16[24,1024]{1,0:T(8,128)(2,1)S(1)} %get-tuple-element.69), channel_id=1, source_target_pairs={{0,96},{1,97},{2,98},{3,99},{4,100},{5,101},{6,102},{7,103},{8,104... | collective-permute-start | bytes 147464 | tf_op jit(solution)/shard_map/ppermute | solution.py:29
  5.1 5.6 %collective-permute-start.1 = (bf16[24,1024]{1,0:T(8,128)(2,1)S(1)}, bf16[24,1024]{1,0:T(8,128)(2,1)S(1)}, u32[]{:S(2)}, u32[]{:S(2)}) collective-permute-start(bf16[24,1024]{1,0:T(8,128)(2,1)S(1)} %get-tuple-element.70), channel_id=1, source_target_pairs={{0,64},{1,65},{2,66},{3,67},{4,68},{5,69},{6,70},{7,71},{8,72},{9,... | collective-permute-start | bytes 147464 | tf_op jit(solution)/shard_map/ppermute | solution.py:29
  10.9 8.2 %collective-permute-start.3 = (bf16[96,1024]{1,0:T(8,128)(2,1)S(1)}, bf16[96,1024]{1,0:T(8,128)(2,1)S(1)}, u32[]{:S(2)}, u32[]{:S(2)}) collective-permute-start(bf16[96,1024]{1,0:T(8,128)(2,1)S(1)} %join_y.1.a), channel_id=1, source_target_pairs={{0,6},{1,25},{2,4},{3,27},{4,2},{5,29},{6,0},{7,31},{8,14},{9,17},... | collective-permute-start | bytes 589832 | tf_op jit(solution)/shard_map/ppermute | solution.py:29
  13.7 7.2 %collective-permute-start.4 = (bf16[96,1024]{1,0:T(8,128)(2,1)S(1)}, bf16[96,1024]{1,0:T(8,128)(2,1)S(1)}, u32[]{:S(2)}, u32[]{:S(2)}) collective-permute-start(bf16[96,1024]{1,0:T(8,128)(2,1)S(1)} %join_y.1.a), channel_id=1, source_target_pairs={{0,4},{1,17},{2,6},{3,19},{4,0},{5,21},{6,2},{7,23},{8,12},{9,25},... | collective-permute-start | bytes 589832 | tf_op jit(solution)/shard_map/ppermute | solution.py:29
  14.5 6.4 %collective-permute-start.5 = (bf16[96,1024]{1,0:T(8,128)(2,1)S(1)}, bf16[96,1024]{1,0:T(8,128)(2,1)S(1)}, u32[]{:S(2)}, u32[]{:S(2)}) collective-permute-start(bf16[96,1024]{1,0:T(8,128)(2,1)S(1)} %join_y.1.a), channel_id=1, source_target_pairs={{0,2},{1,9},{2,0},{3,11},{4,6},{5,13},{6,4},{7,15},{8,10},{9,1},{1... | collective-permute-start | bytes 589832 | tf_op jit(solution)/shard_map/ppermute | solution.py:29
  21.0 14.1 %collective-permute-start.7 = (bf16[4,48,1024]{2,1,0:T(8,128)(2,1)S(1)}, bf16[4,48,1024]{2,1,0:T(8,128)(2,1)S(1)}, u32[]{:S(2)}, u32[]{:S(2)}) collective-permute-start(bf16[4,48,1024]{2,1,0:T(8,128)(2,1)S(1)} %get-tuple-element.83.a), channel_id=1, source_target_pairs={{0,24},{1,7},{2,26},{3,5},{4,28},{5,3},{6,30},{7,1},{8,16},{9,15},... | collective-permute-start | bytes 1179656 | tf_op jit(solution)/shard_map/ppermute | solution.py:29
  25.1 10.0 %collective-permute-start.9 = (bf16[4,48,1024]{2,1,0:T(8,128)(2,1)S(1)}, bf16[4,48,1024]{2,1,0:T(8,128)(2,1)S(1)}, u32[]{:S(2)}, u32[]{:S(2)}) collective-permute-start(bf16[4,48,1024]{2,1,0:T(8,128)(2,1)S(1)} %get-tuple-element.83.a), channel_id=1, source_target_pairs={{0,16},{1,5},{2,18},{3,7},{4,20},{5,1},{6,22},{7,3},{8,24},{9,13},... | collective-permute-start | bytes 1179656 | tf_op jit(solution)/shard_map/ppermute | solution.py:29
  25.1 11.0 %collective-permute-start.11 = (bf16[4,48,1024]{2,1,0:T(8,128)(2,1)S(1)}, bf16[4,48,1024]{2,1,0:T(8,128)(2,1)S(1)}, u32[]{:S(2)}, u32[]{:S(2)}) collective-permute-start(bf16[4,48,1024]{2,1,0:T(8,128)(2,1)S(1)} %get-tuple-element.83.a), channel_id=1, source_target_pairs={{0,8},{1,3},{2,10},{3,1},{4,12},{5,7},{6,14},{7,5},{8,0},{9,11},{1... | collective-permute-start | bytes 1179656 | tf_op jit(solution)/shard_map/ppermute | solution.py:29
  26.0 17.4 %collective-permute-start.13 = (bf16[4,48,1024]{2,1,0:T(8,128)(2,1)S(1)}, bf16[4,48,1024]{2,1,0:T(8,128)(2,1)S(1)}, u32[]{:S(2)}, u32[]{:S(2)}) collective-permute-start(bf16[4,48,1024]{2,1,0:T(8,128)(2,1)S(1)} %get-tuple-element.84.a), channel_id=1, source_target_pairs={{0,24},{1,7},{2,26},{3,5},{4,28},{5,3},{6,30},{7,1},{8,16},{9,15},... | collective-permute-start | bytes 1179656 | tf_op jit(solution)/shard_map/ppermute | solution.py:29
  29.2 14.3 %collective-permute-start.14 = (bf16[4,48,1024]{2,1,0:T(8,128)(2,1)S(1)}, bf16[4,48,1024]{2,1,0:T(8,128)(2,1)S(1)}, u32[]{:S(2)}, u32[]{:S(2)}) collective-permute-start(bf16[4,48,1024]{2,1,0:T(8,128)(2,1)S(1)} %get-tuple-element.84.a), channel_id=1, source_target_pairs={{0,16},{1,5},{2,18},{3,7},{4,20},{5,1},{6,22},{7,3},{8,24},{9,13},... | collective-permute-start | bytes 1179656 | tf_op jit(solution)/shard_map/ppermute | solution.py:29
  35.1 10.6 %collective-permute-start.6 = (bf16[4,48,1024]{2,1,0:T(8,128)(2,1)S(1)}, bf16[4,48,1024]{2,1,0:T(8,128)(2,1)S(1)}, u32[]{:S(2)}, u32[]{:S(2)}) collective-permute-start(bf16[4,48,1024]{2,1,0:T(8,128)(2,1)S(1)} %get-tuple-element.83.a), channel_id=1, source_target_pairs={{0,1},{1,0},{2,3},{3,2},{4,5},{5,4},{6,7},{7,6},{8,9},{9,8},{10,11... | collective-permute-start | bytes 1179656 | tf_op jit(solution)/shard_map/ppermute | solution.py:29
  35.1 10.4 %collective-permute-start.15 = (bf16[4,48,1024]{2,1,0:T(8,128)(2,1)S(1)}, bf16[4,48,1024]{2,1,0:T(8,128)(2,1)S(1)}, u32[]{:S(2)}, u32[]{:S(2)}) collective-permute-start(bf16[4,48,1024]{2,1,0:T(8,128)(2,1)S(1)} %get-tuple-element.84.a), channel_id=1, source_target_pairs={{0,8},{1,3},{2,10},{3,1},{4,12},{5,7},{6,14},{7,5},{8,0},{9,11},{1... | collective-permute-start | bytes 1179656 | tf_op jit(solution)/shard_map/ppermute | solution.py:29
  36.0 9.6 %collective-permute-start.8 = (bf16[4,48,1024]{2,1,0:T(8,128)(2,1)S(1)}, bf16[4,48,1024]{2,1,0:T(8,128)(2,1)S(1)}, u32[]{:S(2)}, u32[]{:S(2)}) collective-permute-start(bf16[4,48,1024]{2,1,0:T(8,128)(2,1)S(1)} %collective-permute-done.7.d), channel_id=1, source_target_pairs={{0,1},{1,0},{2,3},{3,2},{4,5},{5,4},{6,7},{7,6},{8,9},{9,8},{10,11... | collective-permute-start | bytes 1179656 | tf_op jit(solution)/shard_map/ppermute | solution.py:29
  52.4 7.5 %collective-permute-start.17 = (bf16[4,4,48,1024]{3,2,1,0:T(8,128)(2,1)S(1)}, bf16[4,4,48,1024]{3,2,1,0:T(8,128)(2,1)S(1)}, u32[]{:S(2)}, u32[]{:S(2)}) collective-permute-start(bf16[4,4,48,1024]{3,2,1,0:T(8,128)(2,1)S(1)} %back_rows_1.1), channel_id=1, source_target_pairs={{0,1},{1,0},{2,3},{3,2},{4,5},{5,4},{6,7},{7,6},{8,9},{9,8},{10,11... | collective-permute-start | bytes 4718600 | tf_op jit(solution)/shard_map/ppermute | solution.py:29
  54.1 12.8 %collective-permute-start.22 = (bf16[4,48,1024]{2,1,0:T(8,128)(2,1)S(1)}, bf16[4,48,1024]{2,1,0:T(8,128)(2,1)S(1)}, u32[]{:S(2)}, u32[]{:S(2)}) collective-permute-start(bf16[4,48,1024]{2,1,0:T(8,128)(2,1)S(1)} %get-tuple-element.100), channel_id=1, source_target_pairs={{0,24},{1,7},{2,26},{3,5},{4,28},{5,3},{6,30},{7,1},{8,16},{9,15},... | collective-permute-start | bytes 1179656 | tf_op jit(solution)/shard_map/ppermute | solution.py:29
  58.9 15.1 %collective-permute-start.23 = (bf16[4,48,1024]{2,1,0:T(8,128)(2,1)S(1)}, bf16[4,48,1024]{2,1,0:T(8,128)(2,1)S(1)}, u32[]{:S(2)}, u32[]{:S(2)}) collective-permute-start(bf16[4,48,1024]{2,1,0:T(8,128)(2,1)S(1)} %get-tuple-element.101), channel_id=1, source_target_pairs={{0,16},{1,5},{2,18},{3,7},{4,20},{5,1},{6,22},{7,3},{8,24},{9,13},... | collective-permute-start | bytes 1179656 | tf_op jit(solution)/shard_map/ppermute | solution.py:29
  59.0 15.0 %collective-permute-start.24 = (bf16[4,48,1024]{2,1,0:T(8,128)(2,1)S(1)}, bf16[4,48,1024]{2,1,0:T(8,128)(2,1)S(1)}, u32[]{:S(2)}, u32[]{:S(2)}) collective-permute-start(bf16[4,48,1024]{2,1,0:T(8,128)(2,1)S(1)} %get-tuple-element.102), channel_id=1, source_target_pairs={{0,8},{1,3},{2,10},{3,1},{4,12},{5,7},{6,14},{7,5},{8,0},{9,11},{1... | collective-permute-start | bytes 1179656 | tf_op jit(solution)/shard_map/ppermute | solution.py:29
  60.2 15.2 %collective-permute-start.18 = (bf16[4,48,1024]{2,1,0:T(8,128)(2,1)S(1)}, bf16[4,48,1024]{2,1,0:T(8,128)(2,1)S(1)}, u32[]{:S(2)}, u32[]{:S(2)}) collective-permute-start(bf16[4,48,1024]{2,1,0:T(8,128)(2,1)S(1)} %get-tuple-element.95), channel_id=1, source_target_pairs={{0,24},{1,7},{2,26},{3,5},{4,28},{5,3},{6,30},{7,1},{8,16},{9,15},... | collective-permute-start | bytes 1179656 | tf_op jit(solution)/shard_map/ppermute | solution.py:29
  63.5 13.2 %collective-permute-start.19 = (bf16[4,48,1024]{2,1,0:T(8,128)(2,1)S(1)}, bf16[4,48,1024]{2,1,0:T(8,128)(2,1)S(1)}, u32[]{:S(2)}, u32[]{:S(2)}) collective-permute-start(bf16[4,48,1024]{2,1,0:T(8,128)(2,1)S(1)} %get-tuple-element.96), channel_id=1, source_target_pairs={{0,16},{1,5},{2,18},{3,7},{4,20},{5,1},{6,22},{7,3},{8,24},{9,13},... | collective-permute-start | bytes 1179656 | tf_op jit(solution)/shard_map/ppermute | solution.py:29
  67.0 11.3 %collective-permute-start.20 = (bf16[4,48,1024]{2,1,0:T(8,128)(2,1)S(1)}, bf16[4,48,1024]{2,1,0:T(8,128)(2,1)S(1)}, u32[]{:S(2)}, u32[]{:S(2)}) collective-permute-start(bf16[4,48,1024]{2,1,0:T(8,128)(2,1)S(1)} %get-tuple-element.97), channel_id=1, source_target_pairs={{0,8},{1,3},{2,10},{3,1},{4,12},{5,7},{6,14},{7,5},{8,0},{9,11},{1... | collective-permute-start | bytes 1179656 | tf_op jit(solution)/shard_map/ppermute | solution.py:29
  78.7 8.1 %collective-permute-start.25 = (bf16[96,1024]{1,0:T(8,128)(2,1)S(1)}, bf16[96,1024]{1,0:T(8,128)(2,1)S(1)}, u32[]{:S(2)}, u32[]{:S(2)}) collective-permute-start(bf16[96,1024]{1,0:T(8,128)(2,1)S(1)} %get-tuple-element.119), channel_id=1, source_target_pairs={{0,6},{1,25},{2,4},{3,27},{4,2},{5,29},{6,0},{7,31},{8,14},{9,17},... | collective-permute-start | bytes 589832 | tf_op jit(solution)/shard_map/ppermute | solution.py:29
  81.5 7.2 %collective-permute-start.26 = (bf16[96,1024]{1,0:T(8,128)(2,1)S(1)}, bf16[96,1024]{1,0:T(8,128)(2,1)S(1)}, u32[]{:S(2)}, u32[]{:S(2)}) collective-permute-start(bf16[96,1024]{1,0:T(8,128)(2,1)S(1)} %get-tuple-element.120), channel_id=1, source_target_pairs={{0,4},{1,17},{2,6},{3,19},{4,0},{5,21},{6,2},{7,23},{8,12},{9,25},... | collective-permute-start | bytes 589832 | tf_op jit(solution)/shard_map/ppermute | solution.py:29
  82.3 6.4 %collective-permute-start.27 = (bf16[96,1024]{1,0:T(8,128)(2,1)S(1)}, bf16[96,1024]{1,0:T(8,128)(2,1)S(1)}, u32[]{:S(2)}, u32[]{:S(2)}) collective-permute-start(bf16[96,1024]{1,0:T(8,128)(2,1)S(1)} %get-tuple-element.121), channel_id=1, source_target_pairs={{0,2},{1,9},{2,0},{3,11},{4,6},{5,13},{6,4},{7,15},{8,10},{9,1},{1... | collective-permute-start | bytes 589832 | tf_op jit(solution)/shard_map/ppermute | solution.py:29
  90.2 5.6 %collective-permute-start.29 = (bf16[24,1024]{1,0:T(8,128)(2,1)S(1)}, bf16[24,1024]{1,0:T(8,128)(2,1)S(1)}, u32[]{:S(2)}, u32[]{:S(2)}) collective-permute-start(bf16[24,1024]{1,0:T(8,128)(2,1)S(1)} %get-tuple-element.124), channel_id=1, source_target_pairs={{0,64},{1,65},{2,66},{3,67},{4,68},{5,69},{6,70},{7,71},{8,72},{9,... | collective-permute-start | bytes 147464 | tf_op jit(solution)/shard_map/ppermute | solution.py:29
  (7 other events, 28.8 us)

commit v3 on v2

--- a/solution.py
+++ b/solution.py
@@ -45,7 +45,7 @@
     return send(value, lambda i: i ^ (mask << (1 if i & 1 else 3)))
 
 
-ORDER = (0, 3, 2, 1)
+ORDER = (0, 2, 3, 1)
 
 
 def exchange(values, over):
@@ -146,7 +146,7 @@
 def join_y(parts):
     total = 4 * PAIR
 
-    def kernel(a, d, c, b, out):
+    def kernel(a, c, d, b, out):
         stacked = jnp.concatenate([p[...].astype(F32) for p in (a, b, c, d)], axis=0).astype(BF16)
         to = lax.broadcasted_iota(jnp.int32, (total, total), 0)
         come = lax.broadcasted_iota(jnp.int32, (total, total), 1)
@@ -172,7 +172,7 @@
 
 
 def join_first(parts):
-    def kernel(a, d, c, b, x_out, cot_out):
+    def kernel(a, c, d, b, x_out, cot_out):
         for m, part in enumerate((a, b, c, d)):
             x_out[m] = part[:BLOCK, :]
             cot_out[m] = part[BLOCK:, :]
@@ -181,7 +181,7 @@
 
 
 def join_second(parts):
-    def kernel(a, d, c, b, out):
+    def kernel(a, c, d, b, out):
         for m, part in enumerate((a, b, c, d)):
             out[m] = part[...]
 
@@ -321,7 +321,7 @@
 
 
 def sum_second(pieces):
-    def kernel(a, d, c, b, *outs):
+    def kernel(a, c, d, b, *outs):
         for m in range(4):
             total = (a[m].astype(F32) + b[m].astype(F32)) + (c[m].astype(F32) + d[m].astype(F32))
             outs[m][...] = total.astype(outs[m].dtype)
@@ -343,7 +343,7 @@
 
 
 def sum_first(blocks):
-    def kernel(a, d, c, b, *outs):
+    def kernel(a, c, d, b, *outs):
         total = (a[...] + b[...].astype(F32)) + (c[...].astype(F32) + d[...].astype(F32))
         for m in range(4):
             halves = [total[half * BLOCK + m * SLOTS :][:SLOTS] for half in range(2)]
@@ -354,7 +354,7 @@
 
 
 def combine(matrix, parts):
-    def kernel(matrix, a, d, c, b, outputs, grads):
+    def kernel(matrix, a, c, d, b, outputs, grads):
         stacked = jnp.concatenate([p[...].astype(F32) for p in (a, b, c, d)], axis=0)
         total = lax.dot_general(
             matrix[...], stacked, TN, precision=lax.Precision.HIGHEST, preferred_element_type=F32
@@ -370,24 +370,26 @@
     tie = lax.optimization_barrier
     payload = exchange(pack(routing, tokens, grad_out), over_y)
     payload, matrix = tie((payload, combine_matrix(routing)))
-    both, (w_both, w_down) = tie(
-        (exchange([join_y(payload)] * 4, over_first), load_weights(w_gate, w_up, w_down))
+    x_quarter, cot_quarter = join_first(exchange([join_y(payload)] * 4, over_first))
+    x_quarters, (w_both, w_down) = tie(
+        (exchange([x_quarter] * 4, over_second), load_weights(w_gate, w_up, w_down))
     )
-    x_quarter, cot_quarter = join_first(both)
-    x_quarters = exchange([x_quarter] * 4, over_second)
     x_mine = join_second(x_quarters)
-    x_theirs = [over_core(x) for x in x_quarters]
+    (part,) = forward(0, x_mine, w_both, None)
+    own, first, *late = x_quarters
+    part, late = tie((part, late))
+    x_theirs = [over_core(x) for x in (own, first, *late)]
     cot_mine = join_second(exchange([cot_quarter] * 4, over_second))
-    (part,) = forward(0, x_mine, w_both, None)
     x_theirs, cot_mine, part = tie((x_theirs, cot_mine, part))
     x_theirs = join_second(x_theirs)
     cot_theirs = over_core(cot_mine)
     gate_up, hidden = forward(1, x_theirs, w_both, part)
     out_theirs = over_core(out_rows(1, hidden, w_down))
     part = backward_hidden(0, cot_mine, w_down, None, None)
+    out_mine, cot_theirs = tie((out_rows(0, hidden, w_down), cot_theirs))
     d_both = backward_hidden(1, cot_theirs, w_down, part, gate_up)
     back_theirs = over_core(back_rows(1, d_both, w_both))
-    out_pieces = exchange(sum_cores(out_rows(0, hidden, w_down), out_theirs), over_second)
+    out_pieces = exchange(sum_cores(out_mine, out_theirs), over_second)
     back_pieces = exchange(sum_cores(back_rows(0, d_both, w_both), back_theirs), over_second)
     grads = weight_grads((x_mine, x_theirs), (cot_mine, cot_theirs), d_both, hidden)
     back_pieces, out_pieces, grads = tie((back_pieces, out_pieces, grads))

time: 97 us -> 94.3 us (0.972)
  waiting for transfers between devices: 35.8 us -> 31.8 us
  starting transfers between devices: 34.7 us -> 36.1 us
    ppermute x31, waiting for transfers between devices: 35.8 us -> 31.8 us  [send(): return lax.ppermute(value, AXES, [(i, flip(i)) for i in range(128)])]
    ppermute x31, starting transfers between devices: 34.7 us -> 36.1 us  [send(): return lax.ppermute(value, AXES, [(i, flip(i)) for i in range(128)])]
  transfers between devices with their start and end apart: 31 -> 31, of which waited for: 16 -> 17; matrix products, arithmetic and copies ran while one was open for 0% -> 0% of each run, Pallas kernels for 23% -> 24%
where the time goes in v3:
time: 94.3 us; the launch traced here: 94.2 us
  starting transfers between devices  36.1 us (38%)
  waiting for transfers between devices  31.8 us (34%)
  Pallas kernels  25.4 us (27%)
    ppermute x31, starting transfers between devices, send(): return lax.ppermute(value, AXES, [(i, flip(i)) for i in range(128)])  36.1 us
    ppermute x31, waiting for transfers between devices, send(): return lax.ppermute(value, AXES, [(i, flip(i)) for i in range(128)])  31.8 us
    pallas_call x23, Pallas kernels, call(): pl.pallas_call(kernel, out_shape=[jax.ShapeDtypeStruct(s, d) if out else...  25.4 us
  transfers between devices with their start and end apart: 31, of which 17 were waited for; matrix products, arithmetic and copies ran while one was open for 0% of the time, Pallas kernels for 24%

profile of v3, /device:TPU:0, one launch (start us, length us, event | category | flops | bytes accessed | tf_op | source)
XLA Modules:
  0.0 94.2 jit_solution(3218693761926699397)
XLA Ops:
  1.9 3.4 %collective-permute-start = (bf16[24,1024]{1,0:T(8,128)(2,1)S(1)}, bf16[24,1024]{1,0:T(8,128)(2,1)S(1)}, u32[]{:S(2)}, u32[]{:S(2)}) collective-permute-start(bf16[24,1024]{1,0:T(8,128)(2,1)S(1)} %get-tuple-element.74), channel_id=1, source_target_pairs={{0,64},{1,65},{2,66},{3,67},{4,68},{5,69},{6,70},{7,71},{8,72},{9,... | collective-permute-start | bytes 147464 | tf_op jit(solution)/shard_map/ppermute | solution.py:29
  7.6 3.0 %collective-permute-done.1.d = bf16[24,1024]{1,0:T(8,128)(2,1)S(1)} collective-permute-done((bf16[24,1024]{1,0:T(8,128)(2,1)S(1)}, bf16[24,1024]{1,0:T(8,128)(2,1)S(1)}, u32[]{:S(2)}, u32[]{:S(2)}) %collective-permute-start.1) | collective-permute-done | bytes 49184 | tf_op jit(solution)/shard_map/ppermute | solution.py:29
  10.8 3.1 %collective-permute-start.3 = (bf16[96,1024]{1,0:T(8,128)(2,1)S(1)}, bf16[96,1024]{1,0:T(8,128)(2,1)S(1)}, u32[]{:S(2)}, u32[]{:S(2)}) collective-permute-start(bf16[96,1024]{1,0:T(8,128)(2,1)S(1)} %join_y.1.a), channel_id=1, source_target_pairs={{0,4},{1,17},{2,6},{3,19},{4,0},{5,21},{6,2},{7,23},{8,12},{9,25},... | collective-permute-start | bytes 589832 | tf_op jit(solution)/shard_map/ppermute | solution.py:29
  15.0 3.0 %collective-permute-done.3.c = bf16[96,1024]{1,0:T(8,128)(2,1)S(1)} collective-permute-done((bf16[96,1024]{1,0:T(8,128)(2,1)S(1)}, bf16[96,1024]{1,0:T(8,128)(2,1)S(1)}, u32[]{:S(2)}, u32[]{:S(2)}) %collective-permute-start.3) | collective-permute-done | bytes 196640 | tf_op jit(solution)/shard_map/ppermute | solution.py:29
  18.0 2.7 %collective-permute-done.4.d = bf16[96,1024]{1,0:T(8,128)(2,1)S(1)} collective-permute-done((bf16[96,1024]{1,0:T(8,128)(2,1)S(1)}, bf16[96,1024]{1,0:T(8,128)(2,1)S(1)}, u32[]{:S(2)}, u32[]{:S(2)}) %collective-permute-start.4) | collective-permute-done | bytes 196640 | tf_op jit(solution)/shard_map/ppermute | solution.py:29
  20.8 4.0 %collective-permute-start.6 = (bf16[4,48,1024]{2,1,0:T(8,128)(2,1)S(1)}, bf16[4,48,1024]{2,1,0:T(8,128)(2,1)S(1)}, u32[]{:S(2)}, u32[]{:S(2)}) collective-permute-start(bf16[4,48,1024]{2,1,0:T(8,128)(2,1)S(1)} %get-tuple-element.85.a), channel_id=1, source_target_pairs={{0,16},{1,5},{2,18},{3,7},{4,20},{5,1},{6,22},{7,3},{8,24},{9,13},... | collective-permute-start | bytes 1179656 | tf_op jit(solution)/shard_map/ppermute | solution.py:29
  25.8 3.7 %collective-permute-start.13 = (bf16[4,48,1024]{2,1,0:T(8,128)(2,1)S(1)}, bf16[4,48,1024]{2,1,0:T(8,128)(2,1)S(1)}, u32[]{:S(2)}, u32[]{:S(2)}) collective-permute-start(bf16[4,48,1024]{2,1,0:T(8,128)(2,1)S(1)} %get-tuple-element.92.a), channel_id=1, source_target_pairs={{0,16},{1,5},{2,18},{3,7},{4,20},{5,1},{6,22},{7,3},{8,24},{9,13},... | collective-permute-start | bytes 1179656 | tf_op jit(solution)/shard_map/ppermute | solution.py:29
  30.2 3.8 %load_weights.1 = (bf16[4096,768]{1,0:T(8,128)(2,1)S(1)}, bf16[384,4096]{1,0:T(8,128)(2,1)S(1)}) custom-call(bf16[1,4096,384]{2,1,0:T(8,128)(2,1)} %wg.1, bf16[1,4096,384]{2,1,0:T(8,128)(2,1)} %wu.1, bf16[1,384,4096]{2,1,0:T(8,128)(2,1)} %wd.1), custom_call_target="tpu_custom_call" | custom-call | tf_op jit(solution)/shard_map/load_weights/pallas_call | solution.py:61
  37.8 1.7 %collective-permute-done.13.c = bf16[4,48,1024]{2,1,0:T(8,128)(2,1)S(1)} collective-permute-done((bf16[4,48,1024]{2,1,0:T(8,128)(2,1)S(1)}, bf16[4,48,1024]{2,1,0:T(8,128)(2,1)S(1)}, u32[]{:S(2)}, u32[]{:S(2)}) %collective-permute-start.13) | collective-permute-done | bytes 393248 | tf_op jit(solution)/shard_map/ppermute | solution.py:29
  39.6 3.6 %collective-permute-done.14.d = bf16[4,48,1024]{2,1,0:T(8,128)(2,1)S(1)} collective-permute-done((bf16[4,48,1024]{2,1,0:T(8,128)(2,1)S(1)}, bf16[4,48,1024]{2,1,0:T(8,128)(2,1)S(1)}, u32[]{:S(2)}, u32[]{:S(2)}) %collective-permute-start.14) | collective-permute-done | bytes 393248 | tf_op jit(solution)/shard_map/ppermute | solution.py:29
  45.1 1.4 %forward_1.1 = (f32[384,768]{1,0:T(8,128)S(1)}, bf16[384,384]{1,0:T(8,128)(2,1)S(1)}) custom-call(bf16[4,4,48,1024]{3,2,1,0:T(8,128)(2,1)S(1)} %join_second.5.pieces.x_theirs, bf16[4096,768]{1,0:T(8,128)(2,1)S(1)} %get-tuple-element.89.w, f32[384,768]{1,0:T(8,128)S(1)} %forward_0.1.refs_0_), custom_call_target="tpu_custom_call" | custom-call | tf_op jit(solution)/shard_map/forward_1/pallas_call | solution.py:61
  51.1 1.4 %back_rows_1.1 = bf16[4,4,48,1024]{3,2,1,0:T(8,128)(2,1)S(1)} custom-call(bf16[384,768]{1,0:T(8,128)(2,1)S(1)} %backward_hidden_1.1.d, bf16[4096,768]{1,0:T(8,128)(2,1)S(1)} %get-tuple-element.89.w), custom_call_target="tpu_custom_call" | custom-call | tf_op jit(solution)/shard_map/back_rows_1/pallas_call | solution.py:61
  53.3 3.2 %collective-permute-start.22 = (bf16[4,48,1024]{2,1,0:T(8,128)(2,1)S(1)}, bf16[4,48,1024]{2,1,0:T(8,128)(2,1)S(1)}, u32[]{:S(2)}, u32[]{:S(2)}) collective-permute-start(bf16[4,48,1024]{2,1,0:T(8,128)(2,1)S(1)} %get-tuple-element.110), channel_id=1, source_target_pairs={{0,16},{1,5},{2,18},{3,7},{4,20},{5,1},{6,22},{7,3},{8,24},{9,13},... | collective-permute-start | bytes 1179656 | tf_op jit(solution)/shard_map/ppermute | solution.py:29
  56.4 1.4 %back_rows_0.1.a = bf16[4,4,48,1024]{3,2,1,0:T(8,128)(2,1)S(1)} custom-call(bf16[384,768]{1,0:T(8,128)(2,1)S(1)} %backward_hidden_1.1.d, bf16[4096,768]{1,0:T(8,128)(2,1)S(1)} %get-tuple-element.89.w), custom_call_target="tpu_custom_call" | custom-call | tf_op jit(solution)/shard_map/back_rows_0/pallas_call | solution.py:61
  59.9 3.2 %collective-permute-start.18 = (bf16[4,48,1024]{2,1,0:T(8,128)(2,1)S(1)}, bf16[4,48,1024]{2,1,0:T(8,128)(2,1)S(1)}, u32[]{:S(2)}, u32[]{:S(2)}) collective-permute-start(bf16[4,48,1024]{2,1,0:T(8,128)(2,1)S(1)} %get-tuple-element.105), channel_id=1, source_target_pairs={{0,16},{1,5},{2,18},{3,7},{4,20},{5,1},{6,22},{7,3},{8,24},{9,13},... | collective-permute-start | bytes 1179656 | tf_op jit(solution)/shard_map/ppermute | solution.py:29
  64.3 7.0 %weight_grads.1 = (bf16[1,4096,384]{2,1,0:T(8,128)(2,1)}, bf16[1,4096,384]{2,1,0:T(8,128)(2,1)}, bf16[1,384,4096]{2,1,0:T(8,128)(2,1)}) custom-call(bf16[4,4,48,1024]{3,2,1,0:T(8,128)(2,1)S(1)} %join_second.3.pieces.x_mine, bf16[4,4,48,1024]{3,2,1,0:T(8,128)(2,1)S(1)} %join_second.5.pieces.x_theirs, bf16[4,4,48,1024]{3,2,1,0:T(8,128)(2,1)S(1)} %join_second.4.pieces.cot_mine, ...), custom_call_target="tpu_custom_call" | custom-call | tf_op jit(solution)/shard_map/weight_grads/pallas_call | solution.py:61
  71.3 1.4 %collective-permute-done.18.refs_5_ = bf16[4,48,1024]{2,1,0:T(8,128)(2,1)S(1)} collective-permute-done((bf16[4,48,1024]{2,1,0:T(8,128)(2,1)S(1)}, bf16[4,48,1024]{2,1,0:T(8,128)(2,1)S(1)}, u32[]{:S(2)}, u32[]{:S(2)}) %collective-permute-start.18) | collective-permute-done | bytes 393248 | tf_op jit(solution)/shard_map/ppermute | solution.py:29
  72.7 3.6 %collective-permute-done.19.refs_6_ = bf16[4,48,1024]{2,1,0:T(8,128)(2,1)S(1)} collective-permute-done((bf16[4,48,1024]{2,1,0:T(8,128)(2,1)S(1)}, bf16[4,48,1024]{2,1,0:T(8,128)(2,1)S(1)}, u32[]{:S(2)}, u32[]{:S(2)}) %collective-permute-start.19) | collective-permute-done | bytes 393248 | tf_op jit(solution)/shard_map/ppermute | solution.py:29
  76.8 1.6 %collective-permute-start.25 = (bf16[96,1024]{1,0:T(8,128)(2,1)S(1)}, bf16[96,1024]{1,0:T(8,128)(2,1)S(1)}, u32[]{:S(2)}, u32[]{:S(2)}) collective-permute-start(bf16[96,1024]{1,0:T(8,128)(2,1)S(1)} %get-tuple-element.129), channel_id=1, source_target_pairs={{0,4},{1,17},{2,6},{3,19},{4,0},{5,21},{6,2},{7,23},{8,12},{9,25},... | collective-permute-start | bytes 589832 | tf_op jit(solution)/shard_map/ppermute | solution.py:29
  78.4 2.1 %collective-permute-start.26 = (bf16[96,1024]{1,0:T(8,128)(2,1)S(1)}, bf16[96,1024]{1,0:T(8,128)(2,1)S(1)}, u32[]{:S(2)}, u32[]{:S(2)}) collective-permute-start(bf16[96,1024]{1,0:T(8,128)(2,1)S(1)} %get-tuple-element.130), channel_id=1, source_target_pairs={{0,6},{1,25},{2,4},{3,27},{4,2},{5,29},{6,0},{7,31},{8,14},{9,17},... | collective-permute-start | bytes 589832 | tf_op jit(solution)/shard_map/ppermute | solution.py:29
  80.5 3.6 %collective-permute-done.25.c = bf16[96,1024]{1,0:T(8,128)(2,1)S(1)} collective-permute-done((bf16[96,1024]{1,0:T(8,128)(2,1)S(1)}, bf16[96,1024]{1,0:T(8,128)(2,1)S(1)}, u32[]{:S(2)}, u32[]{:S(2)}) %collective-permute-start.25) | collective-permute-done | bytes 196640 | tf_op jit(solution)/shard_map/ppermute | solution.py:29
  84.1 2.0 %collective-permute-done.26.d = bf16[96,1024]{1,0:T(8,128)(2,1)S(1)} collective-permute-done((bf16[96,1024]{1,0:T(8,128)(2,1)S(1)}, bf16[96,1024]{1,0:T(8,128)(2,1)S(1)}, u32[]{:S(2)}, u32[]{:S(2)}) %collective-permute-start.26) | collective-permute-done | bytes 196640 | tf_op jit(solution)/shard_map/ppermute | solution.py:29
  86.3 1.6 %collective-permute-start.28 = (bf16[24,1024]{1,0:T(8,128)(2,1)S(1)}, bf16[24,1024]{1,0:T(8,128)(2,1)S(1)}, u32[]{:S(2)}, u32[]{:S(2)}) collective-permute-start(bf16[24,1024]{1,0:T(8,128)(2,1)S(1)} %get-tuple-element.133), channel_id=1, source_target_pairs={{0,64},{1,65},{2,66},{3,67},{4,68},{5,69},{6,70},{7,71},{8,72},{9,... | collective-permute-start | bytes 147464 | tf_op jit(solution)/shard_map/ppermute | solution.py:29
  89.8 2.4 %collective-permute-done.28.c = bf16[24,1024]{1,0:T(8,128)(2,1)S(1)} collective-permute-done((bf16[24,1024]{1,0:T(8,128)(2,1)S(1)}, bf16[24,1024]{1,0:T(8,128)(2,1)S(1)}, u32[]{:S(2)}, u32[]{:S(2)}) %collective-permute-start.28) | collective-permute-done | bytes 49184 | tf_op jit(solution)/shard_map/ppermute | solution.py:29
  (61 shorter events, 25.4 us)
Async XLA Ops:
  1.9 5.7 %collective-permute-start = (bf16[24,1024]{1,0:T(8,128)(2,1)S(1)}, bf16[24,1024]{1,0:T(8,128)(2,1)S(1)}, u32[]{:S(2)}, u32[]{:S(2)}) collective-permute-start(bf16[24,1024]{1,0:T(8,128)(2,1)S(1)} %get-tuple-element.74), channel_id=1, source_target_pairs={{0,64},{1,65},{2,66},{3,67},{4,68},{5,69},{6,70},{7,71},{8,72},{9,... | collective-permute-start | bytes 147464 | tf_op jit(solution)/shard_map/ppermute | solution.py:29
  10.8 7.3 %collective-permute-start.3 = (bf16[96,1024]{1,0:T(8,128)(2,1)S(1)}, bf16[96,1024]{1,0:T(8,128)(2,1)S(1)}, u32[]{:S(2)}, u32[]{:S(2)}) collective-permute-start(bf16[96,1024]{1,0:T(8,128)(2,1)S(1)} %join_y.1.a), channel_id=1, source_target_pairs={{0,4},{1,17},{2,6},{3,19},{4,0},{5,21},{6,2},{7,23},{8,12},{9,25},... | collective-permute-start | bytes 589832 | tf_op jit(solution)/shard_map/ppermute | solution.py:29
  13.9 6.9 %collective-permute-start.4 = (bf16[96,1024]{1,0:T(8,128)(2,1)S(1)}, bf16[96,1024]{1,0:T(8,128)(2,1)S(1)}, u32[]{:S(2)}, u32[]{:S(2)}) collective-permute-start(bf16[96,1024]{1,0:T(8,128)(2,1)S(1)} %join_y.1.a), channel_id=1, source_target_pairs={{0,6},{1,25},{2,4},{3,27},{4,2},{5,29},{6,0},{7,31},{8,14},{9,17},... | collective-permute-start | bytes 589832 | tf_op jit(solution)/shard_map/ppermute | solution.py:29
  15.0 5.7 %collective-permute-start.5 = (bf16[96,1024]{1,0:T(8,128)(2,1)S(1)}, bf16[96,1024]{1,0:T(8,128)(2,1)S(1)}, u32[]{:S(2)}, u32[]{:S(2)}) collective-permute-start(bf16[96,1024]{1,0:T(8,128)(2,1)S(1)} %join_y.1.a), channel_id=1, source_target_pairs={{0,2},{1,9},{2,0},{3,11},{4,6},{5,13},{6,4},{7,15},{8,10},{9,1},{1... | collective-permute-start | bytes 589832 | tf_op jit(solution)/shard_map/ppermute | solution.py:29
  20.8 13.2 %collective-permute-start.6 = (bf16[4,48,1024]{2,1,0:T(8,128)(2,1)S(1)}, bf16[4,48,1024]{2,1,0:T(8,128)(2,1)S(1)}, u32[]{:S(2)}, u32[]{:S(2)}) collective-permute-start(bf16[4,48,1024]{2,1,0:T(8,128)(2,1)S(1)} %get-tuple-element.85.a), channel_id=1, source_target_pairs={{0,16},{1,5},{2,18},{3,7},{4,20},{5,1},{6,22},{7,3},{8,24},{9,13},... | collective-permute-start | bytes 1179656 | tf_op jit(solution)/shard_map/ppermute | solution.py:29
  24.8 10.0 %collective-permute-start.7 = (bf16[4,48,1024]{2,1,0:T(8,128)(2,1)S(1)}, bf16[4,48,1024]{2,1,0:T(8,128)(2,1)S(1)}, u32[]{:S(2)}, u32[]{:S(2)}) collective-permute-start(bf16[4,48,1024]{2,1,0:T(8,128)(2,1)S(1)} %get-tuple-element.85.a), channel_id=1, source_target_pairs={{0,24},{1,7},{2,26},{3,5},{4,28},{5,3},{6,30},{7,1},{8,16},{9,15},... | collective-permute-start | bytes 1179656 | tf_op jit(solution)/shard_map/ppermute | solution.py:29
  25.5 10.3 %collective-permute-start.8 = (bf16[4,48,1024]{2,1,0:T(8,128)(2,1)S(1)}, bf16[4,48,1024]{2,1,0:T(8,128)(2,1)S(1)}, u32[]{:S(2)}, u32[]{:S(2)}) collective-permute-start(bf16[4,48,1024]{2,1,0:T(8,128)(2,1)S(1)} %get-tuple-element.85.a), channel_id=1, source_target_pairs={{0,8},{1,3},{2,10},{3,1},{4,12},{5,7},{6,14},{7,5},{8,0},{9,11},{1... | collective-permute-start | bytes 1179656 | tf_op jit(solution)/shard_map/ppermute | solution.py:29
  25.8 13.7 %collective-permute-start.13 = (bf16[4,48,1024]{2,1,0:T(8,128)(2,1)S(1)}, bf16[4,48,1024]{2,1,0:T(8,128)(2,1)S(1)}, u32[]{:S(2)}, u32[]{:S(2)}) collective-permute-start(bf16[4,48,1024]{2,1,0:T(8,128)(2,1)S(1)} %get-tuple-element.92.a), channel_id=1, source_target_pairs={{0,16},{1,5},{2,18},{3,7},{4,20},{5,1},{6,22},{7,3},{8,24},{9,13},... | collective-permute-start | bytes 1179656 | tf_op jit(solution)/shard_map/ppermute | solution.py:29
  29.5 13.7 %collective-permute-start.14 = (bf16[4,48,1024]{2,1,0:T(8,128)(2,1)S(1)}, bf16[4,48,1024]{2,1,0:T(8,128)(2,1)S(1)}, u32[]{:S(2)}, u32[]{:S(2)}) collective-permute-start(bf16[4,48,1024]{2,1,0:T(8,128)(2,1)S(1)} %get-tuple-element.92.a), channel_id=1, source_target_pairs={{0,24},{1,7},{2,26},{3,5},{4,28},{5,3},{6,30},{7,1},{8,16},{9,15},... | collective-permute-start | bytes 1179656 | tf_op jit(solution)/shard_map/ppermute | solution.py:29
  34.0 10.3 %collective-permute-start.15 = (bf16[4,48,1024]{2,1,0:T(8,128)(2,1)S(1)}, bf16[4,48,1024]{2,1,0:T(8,128)(2,1)S(1)}, u32[]{:S(2)}, u32[]{:S(2)}) collective-permute-start(bf16[4,48,1024]{2,1,0:T(8,128)(2,1)S(1)} %get-tuple-element.92.a), channel_id=1, source_target_pairs={{0,8},{1,3},{2,10},{3,1},{4,12},{5,7},{6,14},{7,5},{8,0},{9,11},{1... | collective-permute-start | bytes 1179656 | tf_op jit(solution)/shard_map/ppermute | solution.py:29
  35.8 8.6 %collective-permute-start.9 = (bf16[4,48,1024]{2,1,0:T(8,128)(2,1)S(1)}, bf16[4,48,1024]{2,1,0:T(8,128)(2,1)S(1)}, u32[]{:S(2)}, u32[]{:S(2)}) collective-permute-start(bf16[4,48,1024]{2,1,0:T(8,128)(2,1)S(1)} %get-tuple-element.85.a), channel_id=1, source_target_pairs={{0,1},{1,0},{2,3},{3,2},{4,5},{5,4},{6,7},{7,6},{8,9},{9,8},{10,11... | collective-permute-start | bytes 1179656 | tf_op jit(solution)/shard_map/ppermute | solution.py:29
  35.8 8.6 %collective-permute-start.10 = (bf16[4,48,1024]{2,1,0:T(8,128)(2,1)S(1)}, bf16[4,48,1024]{2,1,0:T(8,128)(2,1)S(1)}, u32[]{:S(2)}, u32[]{:S(2)}) collective-permute-start(bf16[4,48,1024]{2,1,0:T(8,128)(2,1)S(1)} %collective-permute-done.6.c), channel_id=1, source_target_pairs={{0,1},{1,0},{2,3},{3,2},{4,5},{5,4},{6,7},{7,6},{8,9},{9,8},{10,11... | collective-permute-start | bytes 1179656 | tf_op jit(solution)/shard_map/ppermute | solution.py:29
  47.5 5.4 %collective-permute-start.21 = (bf16[4,4,48,1024]{3,2,1,0:T(8,128)(2,1)S(1)}, bf16[4,4,48,1024]{3,2,1,0:T(8,128)(2,1)S(1)}, u32[]{:S(2)}, u32[]{:S(2)}) collective-permute-start(bf16[4,4,48,1024]{3,2,1,0:T(8,128)(2,1)S(1)} %out_rows_1.1), channel_id=1, source_target_pairs={{0,1},{1,0},{2,3},{3,2},{4,5},{5,4},{6,7},{7,6},{8,9},{9,8},{10,11... | collective-permute-start | bytes 4718600 | tf_op jit(solution)/shard_map/ppermute | solution.py:29
  52.5 7.0 %collective-permute-start.17 = (bf16[4,4,48,1024]{3,2,1,0:T(8,128)(2,1)S(1)}, bf16[4,4,48,1024]{3,2,1,0:T(8,128)(2,1)S(1)}, u32[]{:S(2)}, u32[]{:S(2)}) collective-permute-start(bf16[4,4,48,1024]{3,2,1,0:T(8,128)(2,1)S(1)} %back_rows_1.1), channel_id=1, source_target_pairs={{0,1},{1,0},{2,3},{3,2},{4,5},{5,4},{6,7},{7,6},{8,9},{9,8},{10,11... | collective-permute-start | bytes 4718600 | tf_op jit(solution)/shard_map/ppermute | solution.py:29
  53.3 11.0 %collective-permute-start.22 = (bf16[4,48,1024]{2,1,0:T(8,128)(2,1)S(1)}, bf16[4,48,1024]{2,1,0:T(8,128)(2,1)S(1)}, u32[]{:S(2)}, u32[]{:S(2)}) collective-permute-start(bf16[4,48,1024]{2,1,0:T(8,128)(2,1)S(1)} %get-tuple-element.110), channel_id=1, source_target_pairs={{0,16},{1,5},{2,18},{3,7},{4,20},{5,1},{6,22},{7,3},{8,24},{9,13},... | collective-permute-start | bytes 1179656 | tf_op jit(solution)/shard_map/ppermute | solution.py:29
  57.9 13.4 %collective-permute-start.23 = (bf16[4,48,1024]{2,1,0:T(8,128)(2,1)S(1)}, bf16[4,48,1024]{2,1,0:T(8,128)(2,1)S(1)}, u32[]{:S(2)}, u32[]{:S(2)}) collective-permute-start(bf16[4,48,1024]{2,1,0:T(8,128)(2,1)S(1)} %get-tuple-element.111), channel_id=1, source_target_pairs={{0,24},{1,7},{2,26},{3,5},{4,28},{5,3},{6,30},{7,1},{8,16},{9,15},... | collective-permute-start | bytes 1179656 | tf_op jit(solution)/shard_map/ppermute | solution.py:29
  59.1 12.2 %collective-permute-start.24 = (bf16[4,48,1024]{2,1,0:T(8,128)(2,1)S(1)}, bf16[4,48,1024]{2,1,0:T(8,128)(2,1)S(1)}, u32[]{:S(2)}, u32[]{:S(2)}) collective-permute-start(bf16[4,48,1024]{2,1,0:T(8,128)(2,1)S(1)} %get-tuple-element.112), channel_id=1, source_target_pairs={{0,8},{1,3},{2,10},{3,1},{4,12},{5,7},{6,14},{7,5},{8,0},{9,11},{1... | collective-permute-start | bytes 1179656 | tf_op jit(solution)/shard_map/ppermute | solution.py:29
  59.9 12.9 %collective-permute-start.18 = (bf16[4,48,1024]{2,1,0:T(8,128)(2,1)S(1)}, bf16[4,48,1024]{2,1,0:T(8,128)(2,1)S(1)}, u32[]{:S(2)}, u32[]{:S(2)}) collective-permute-start(bf16[4,48,1024]{2,1,0:T(8,128)(2,1)S(1)} %get-tuple-element.105), channel_id=1, source_target_pairs={{0,16},{1,5},{2,18},{3,7},{4,20},{5,1},{6,22},{7,3},{8,24},{9,13},... | collective-permute-start | bytes 1179656 | tf_op jit(solution)/shard_map/ppermute | solution.py:29
  63.1 13.2 %collective-permute-start.19 = (bf16[4,48,1024]{2,1,0:T(8,128)(2,1)S(1)}, bf16[4,48,1024]{2,1,0:T(8,128)(2,1)S(1)}, u32[]{:S(2)}, u32[]{:S(2)}) collective-permute-start(bf16[4,48,1024]{2,1,0:T(8,128)(2,1)S(1)} %get-tuple-element.106), channel_id=1, source_target_pairs={{0,24},{1,7},{2,26},{3,5},{4,28},{5,3},{6,30},{7,1},{8,16},{9,15},... | collective-permute-start | bytes 1179656 | tf_op jit(solution)/shard_map/ppermute | solution.py:29
  64.2 12.1 %collective-permute-start.20 = (bf16[4,48,1024]{2,1,0:T(8,128)(2,1)S(1)}, bf16[4,48,1024]{2,1,0:T(8,128)(2,1)S(1)}, u32[]{:S(2)}, u32[]{:S(2)}) collective-permute-start(bf16[4,48,1024]{2,1,0:T(8,128)(2,1)S(1)} %get-tuple-element.107), channel_id=1, source_target_pairs={{0,8},{1,3},{2,10},{3,1},{4,12},{5,7},{6,14},{7,5},{8,0},{9,11},{1... | collective-permute-start | bytes 1179656 | tf_op jit(solution)/shard_map/ppermute | solution.py:29
  76.8 7.3 %collective-permute-start.25 = (bf16[96,1024]{1,0:T(8,128)(2,1)S(1)}, bf16[96,1024]{1,0:T(8,128)(2,1)S(1)}, u32[]{:S(2)}, u32[]{:S(2)}) collective-permute-start(bf16[96,1024]{1,0:T(8,128)(2,1)S(1)} %get-tuple-element.129), channel_id=1, source_target_pairs={{0,4},{1,17},{2,6},{3,19},{4,0},{5,21},{6,2},{7,23},{8,12},{9,25},... | collective-permute-start | bytes 589832 | tf_op jit(solution)/shard_map/ppermute | solution.py:29
  78.4 7.7 %collective-permute-start.26 = (bf16[96,1024]{1,0:T(8,128)(2,1)S(1)}, bf16[96,1024]{1,0:T(8,128)(2,1)S(1)}, u32[]{:S(2)}, u32[]{:S(2)}) collective-permute-start(bf16[96,1024]{1,0:T(8,128)(2,1)S(1)} %get-tuple-element.130), channel_id=1, source_target_pairs={{0,6},{1,25},{2,4},{3,27},{4,2},{5,29},{6,0},{7,31},{8,14},{9,17},... | collective-permute-start | bytes 589832 | tf_op jit(solution)/shard_map/ppermute | solution.py:29
  80.5 5.7 %collective-permute-start.27 = (bf16[96,1024]{1,0:T(8,128)(2,1)S(1)}, bf16[96,1024]{1,0:T(8,128)(2,1)S(1)}, u32[]{:S(2)}, u32[]{:S(2)}) collective-permute-start(bf16[96,1024]{1,0:T(8,128)(2,1)S(1)} %get-tuple-element.131), channel_id=1, source_target_pairs={{0,2},{1,9},{2,0},{3,11},{4,6},{5,13},{6,4},{7,15},{8,10},{9,1},{1... | collective-permute-start | bytes 589832 | tf_op jit(solution)/shard_map/ppermute | solution.py:29
  86.3 6.0 %collective-permute-start.28 = (bf16[24,1024]{1,0:T(8,128)(2,1)S(1)}, bf16[24,1024]{1,0:T(8,128)(2,1)S(1)}, u32[]{:S(2)}, u32[]{:S(2)}) collective-permute-start(bf16[24,1024]{1,0:T(8,128)(2,1)S(1)} %get-tuple-element.133), channel_id=1, source_target_pairs={{0,64},{1,65},{2,66},{3,67},{4,68},{5,69},{6,70},{7,71},{8,72},{9,... | collective-permute-start | bytes 147464 | tf_op jit(solution)/shard_map/ppermute | solution.py:29
  (7 other events, 30.8 us)

commit v4 on v3

--- a/solution.py
+++ b/solution.py
@@ -117,10 +117,11 @@
     def kernel(*refs):
         sources, outs, (counts, hosted, picks, gates, values, sems) = refs[:6], refs[6:10], refs[10:]
         targets = [counts, hosted, picks, gates, values.at[:TOK], values.at[TOK:]]
-        for copy in fetch(sources, targets, sems):
-            copy.wait()
+        copies = fetch(sources, targets, sems)
+        wait_all(copies[:4])
         one_hot, late, weight = slots_of(counts, hosted, picks[...], gates[...])
         scale = jnp.sum(jnp.where(late, one_hot * weight, one_hot), axis=1, keepdims=True)
+        wait_all(copies[4:])
         rows = jnp.dot(one_hot.astype(BF16), values[...], preferred_element_type=F32) * scale
         for m in range(4):
             outs[m][...] = rows[m * PAIR : (m + 1) * PAIR].astype(BF16)
@@ -386,7 +387,7 @@
     gate_up, hidden = forward(1, x_theirs, w_both, part)
     out_theirs = over_core(out_rows(1, hidden, w_down))
     part = backward_hidden(0, cot_mine, w_down, None, None)
-    out_mine, cot_theirs = tie((out_rows(0, hidden, w_down), cot_theirs))
+    out_mine = out_rows(0, hidden, w_down)
     d_both = backward_hidden(1, cot_theirs, w_down, part, gate_up)
     back_theirs = over_core(back_rows(1, d_both, w_both))
     out_pieces = exchange(sum_cores(out_mine, out_theirs), over_second)

time: 94.3 us -> 94.3 us (level)
  no operation moved by 1% of the time
where the time goes in v4:
time: 94.3 us; the launch traced here: 94.2 us
  starting transfers between devices  36.1 us (38%)
  waiting for transfers between devices  31.8 us (34%)
  Pallas kernels  25.4 us (27%)
    ppermute x31, starting transfers between devices, send(): return lax.ppermute(value, AXES, [(i, flip(i)) for i in range(128)])  36.1 us
    ppermute x31, waiting for transfers between devices, send(): return lax.ppermute(value, AXES, [(i, flip(i)) for i in range(128)])  31.8 us
    pallas_call x23, Pallas kernels, call(): pl.pallas_call(kernel, out_shape=[jax.ShapeDtypeStruct(s, d) if out else...  25.4 us
  transfers between devices with their start and end apart: 31, of which 17 were waited for; matrix products, arithmetic and copies ran while one was open for 0% of the time, Pallas kernels for 24%

profile of v4, /device:TPU:0, one launch (start us, length us, event | category | flops | bytes accessed | tf_op | source)
XLA Modules:
  0.0 94.2 jit_solution(8958319892367330871)
XLA Ops:
  1.9 3.4 %collective-permute-start = (bf16[24,1024]{1,0:T(8,128)(2,1)S(1)}, bf16[24,1024]{1,0:T(8,128)(2,1)S(1)}, u32[]{:S(2)}, u32[]{:S(2)}) collective-permute-start(bf16[24,1024]{1,0:T(8,128)(2,1)S(1)} %get-tuple-element.72), channel_id=1, source_target_pairs={{0,64},{1,65},{2,66},{3,67},{4,68},{5,69},{6,70},{7,71},{8,72},{9,... | collective-permute-start | bytes 147464 | tf_op jit(solution)/shard_map/ppermute | solution.py:29
  7.6 3.0 %collective-permute-done.1.d = bf16[24,1024]{1,0:T(8,128)(2,1)S(1)} collective-permute-done((bf16[24,1024]{1,0:T(8,128)(2,1)S(1)}, bf16[24,1024]{1,0:T(8,128)(2,1)S(1)}, u32[]{:S(2)}, u32[]{:S(2)}) %collective-permute-start.1) | collective-permute-done | bytes 49184 | tf_op jit(solution)/shard_map/ppermute | solution.py:29
  10.8 3.1 %collective-permute-start.3 = (bf16[96,1024]{1,0:T(8,128)(2,1)S(1)}, bf16[96,1024]{1,0:T(8,128)(2,1)S(1)}, u32[]{:S(2)}, u32[]{:S(2)}) collective-permute-start(bf16[96,1024]{1,0:T(8,128)(2,1)S(1)} %join_y.1.a), channel_id=1, source_target_pairs={{0,4},{1,17},{2,6},{3,19},{4,0},{5,21},{6,2},{7,23},{8,12},{9,25},... | collective-permute-start | bytes 589832 | tf_op jit(solution)/shard_map/ppermute | solution.py:29
  15.0 3.0 %collective-permute-done.3.c = bf16[96,1024]{1,0:T(8,128)(2,1)S(1)} collective-permute-done((bf16[96,1024]{1,0:T(8,128)(2,1)S(1)}, bf16[96,1024]{1,0:T(8,128)(2,1)S(1)}, u32[]{:S(2)}, u32[]{:S(2)}) %collective-permute-start.3) | collective-permute-done | bytes 196640 | tf_op jit(solution)/shard_map/ppermute | solution.py:29
  18.0 2.7 %collective-permute-done.4.d = bf16[96,1024]{1,0:T(8,128)(2,1)S(1)} collective-permute-done((bf16[96,1024]{1,0:T(8,128)(2,1)S(1)}, bf16[96,1024]{1,0:T(8,128)(2,1)S(1)}, u32[]{:S(2)}, u32[]{:S(2)}) %collective-permute-start.4) | collective-permute-done | bytes 196640 | tf_op jit(solution)/shard_map/ppermute | solution.py:29
  20.8 4.0 %collective-permute-start.6 = (bf16[4,48,1024]{2,1,0:T(8,128)(2,1)S(1)}, bf16[4,48,1024]{2,1,0:T(8,128)(2,1)S(1)}, u32[]{:S(2)}, u32[]{:S(2)}) collective-permute-start(bf16[4,48,1024]{2,1,0:T(8,128)(2,1)S(1)} %get-tuple-element.83.a), channel_id=1, source_target_pairs={{0,16},{1,5},{2,18},{3,7},{4,20},{5,1},{6,22},{7,3},{8,24},{9,13},... | collective-permute-start | bytes 1179656 | tf_op jit(solution)/shard_map/ppermute | solution.py:29
  25.8 3.7 %collective-permute-start.13 = (bf16[4,48,1024]{2,1,0:T(8,128)(2,1)S(1)}, bf16[4,48,1024]{2,1,0:T(8,128)(2,1)S(1)}, u32[]{:S(2)}, u32[]{:S(2)}) collective-permute-start(bf16[4,48,1024]{2,1,0:T(8,128)(2,1)S(1)} %get-tuple-element.90.a), channel_id=1, source_target_pairs={{0,16},{1,5},{2,18},{3,7},{4,20},{5,1},{6,22},{7,3},{8,24},{9,13},... | collective-permute-start | bytes 1179656 | tf_op jit(solution)/shard_map/ppermute | solution.py:29
  30.2 3.8 %load_weights.1 = (bf16[4096,768]{1,0:T(8,128)(2,1)S(1)}, bf16[384,4096]{1,0:T(8,128)(2,1)S(1)}) custom-call(bf16[1,4096,384]{2,1,0:T(8,128)(2,1)} %wg.1, bf16[1,4096,384]{2,1,0:T(8,128)(2,1)} %wu.1, bf16[1,384,4096]{2,1,0:T(8,128)(2,1)} %wd.1), custom_call_target="tpu_custom_call" | custom-call | tf_op jit(solution)/shard_map/load_weights/pallas_call | solution.py:61
  37.8 1.7 %collective-permute-done.13.c = bf16[4,48,1024]{2,1,0:T(8,128)(2,1)S(1)} collective-permute-done((bf16[4,48,1024]{2,1,0:T(8,128)(2,1)S(1)}, bf16[4,48,1024]{2,1,0:T(8,128)(2,1)S(1)}, u32[]{:S(2)}, u32[]{:S(2)}) %collective-permute-start.13) | collective-permute-done | bytes 393248 | tf_op jit(solution)/shard_map/ppermute | solution.py:29
  39.5 3.6 %collective-permute-done.14.d = bf16[4,48,1024]{2,1,0:T(8,128)(2,1)S(1)} collective-permute-done((bf16[4,48,1024]{2,1,0:T(8,128)(2,1)S(1)}, bf16[4,48,1024]{2,1,0:T(8,128)(2,1)S(1)}, u32[]{:S(2)}, u32[]{:S(2)}) %collective-permute-start.14) | collective-permute-done | bytes 393248 | tf_op jit(solution)/shard_map/ppermute | solution.py:29
  45.1 1.4 %forward_1.1 = (f32[384,768]{1,0:T(8,128)S(1)}, bf16[384,384]{1,0:T(8,128)(2,1)S(1)}) custom-call(bf16[4,4,48,1024]{3,2,1,0:T(8,128)(2,1)S(1)} %join_second.5.pieces.x_theirs, bf16[4096,768]{1,0:T(8,128)(2,1)S(1)} %get-tuple-element.87.w, f32[384,768]{1,0:T(8,128)S(1)} %forward_0.1.refs_0_), custom_call_target="tpu_custom_call" | custom-call | tf_op jit(solution)/shard_map/forward_1/pallas_call | solution.py:61
  50.1 1.4 %back_rows_1.1 = bf16[4,4,48,1024]{3,2,1,0:T(8,128)(2,1)S(1)} custom-call(bf16[384,768]{1,0:T(8,128)(2,1)S(1)} %backward_hidden_1.1.d, bf16[4096,768]{1,0:T(8,128)(2,1)S(1)} %get-tuple-element.87.w), custom_call_target="tpu_custom_call" | custom-call | tf_op jit(solution)/shard_map/back_rows_1/pallas_call | solution.py:61
  53.3 3.2 %collective-permute-start.22 = (bf16[4,48,1024]{2,1,0:T(8,128)(2,1)S(1)}, bf16[4,48,1024]{2,1,0:T(8,128)(2,1)S(1)}, u32[]{:S(2)}, u32[]{:S(2)}) collective-permute-start(bf16[4,48,1024]{2,1,0:T(8,128)(2,1)S(1)} %get-tuple-element.106), channel_id=1, source_target_pairs={{0,16},{1,5},{2,18},{3,7},{4,20},{5,1},{6,22},{7,3},{8,24},{9,13},... | collective-permute-start | bytes 1179656 | tf_op jit(solution)/shard_map/ppermute | solution.py:29
  56.4 1.4 %back_rows_0.1.a = bf16[4,4,48,1024]{3,2,1,0:T(8,128)(2,1)S(1)} custom-call(bf16[384,768]{1,0:T(8,128)(2,1)S(1)} %backward_hidden_1.1.d, bf16[4096,768]{1,0:T(8,128)(2,1)S(1)} %get-tuple-element.87.w), custom_call_target="tpu_custom_call" | custom-call | tf_op jit(solution)/shard_map/back_rows_0/pallas_call | solution.py:61
  59.9 3.2 %collective-permute-start.18 = (bf16[4,48,1024]{2,1,0:T(8,128)(2,1)S(1)}, bf16[4,48,1024]{2,1,0:T(8,128)(2,1)S(1)}, u32[]{:S(2)}, u32[]{:S(2)}) collective-permute-start(bf16[4,48,1024]{2,1,0:T(8,128)(2,1)S(1)} %get-tuple-element.101), channel_id=1, source_target_pairs={{0,16},{1,5},{2,18},{3,7},{4,20},{5,1},{6,22},{7,3},{8,24},{9,13},... | collective-permute-start | bytes 1179656 | tf_op jit(solution)/shard_map/ppermute | solution.py:29
  64.3 7.0 %weight_grads.1 = (bf16[1,4096,384]{2,1,0:T(8,128)(2,1)}, bf16[1,4096,384]{2,1,0:T(8,128)(2,1)}, bf16[1,384,4096]{2,1,0:T(8,128)(2,1)}) custom-call(bf16[4,4,48,1024]{3,2,1,0:T(8,128)(2,1)S(1)} %join_second.3.pieces.x_mine, bf16[4,4,48,1024]{3,2,1,0:T(8,128)(2,1)S(1)} %join_second.5.pieces.x_theirs, bf16[4,4,48,1024]{3,2,1,0:T(8,128)(2,1)S(1)} %join_second.4.pieces.cot_mine, ...), custom_call_target="tpu_custom_call" | custom-call | tf_op jit(solution)/shard_map/weight_grads/pallas_call | solution.py:61
  71.3 1.4 %collective-permute-done.18.refs_5_ = bf16[4,48,1024]{2,1,0:T(8,128)(2,1)S(1)} collective-permute-done((bf16[4,48,1024]{2,1,0:T(8,128)(2,1)S(1)}, bf16[4,48,1024]{2,1,0:T(8,128)(2,1)S(1)}, u32[]{:S(2)}, u32[]{:S(2)}) %collective-permute-start.18) | collective-permute-done | bytes 393248 | tf_op jit(solution)/shard_map/ppermute | solution.py:29
  72.7 3.6 %collective-permute-done.19.refs_6_ = bf16[4,48,1024]{2,1,0:T(8,128)(2,1)S(1)} collective-permute-done((bf16[4,48,1024]{2,1,0:T(8,128)(2,1)S(1)}, bf16[4,48,1024]{2,1,0:T(8,128)(2,1)S(1)}, u32[]{:S(2)}, u32[]{:S(2)}) %collective-permute-start.19) | collective-permute-done | bytes 393248 | tf_op jit(solution)/shard_map/ppermute | solution.py:29
  76.8 1.6 %collective-permute-start.25 = (bf16[96,1024]{1,0:T(8,128)(2,1)S(1)}, bf16[96,1024]{1,0:T(8,128)(2,1)S(1)}, u32[]{:S(2)}, u32[]{:S(2)}) collective-permute-start(bf16[96,1024]{1,0:T(8,128)(2,1)S(1)} %get-tuple-element.125), channel_id=1, source_target_pairs={{0,4},{1,17},{2,6},{3,19},{4,0},{5,21},{6,2},{7,23},{8,12},{9,25},... | collective-permute-start | bytes 589832 | tf_op jit(solution)/shard_map/ppermute | solution.py:29
  78.4 2.1 %collective-permute-start.26 = (bf16[96,1024]{1,0:T(8,128)(2,1)S(1)}, bf16[96,1024]{1,0:T(8,128)(2,1)S(1)}, u32[]{:S(2)}, u32[]{:S(2)}) collective-permute-start(bf16[96,1024]{1,0:T(8,128)(2,1)S(1)} %get-tuple-element.126), channel_id=1, source_target_pairs={{0,6},{1,25},{2,4},{3,27},{4,2},{5,29},{6,0},{7,31},{8,14},{9,17},... | collective-permute-start | bytes 589832 | tf_op jit(solution)/shard_map/ppermute | solution.py:29
  80.5 3.6 %collective-permute-done.25.c = bf16[96,1024]{1,0:T(8,128)(2,1)S(1)} collective-permute-done((bf16[96,1024]{1,0:T(8,128)(2,1)S(1)}, bf16[96,1024]{1,0:T(8,128)(2,1)S(1)}, u32[]{:S(2)}, u32[]{:S(2)}) %collective-permute-start.25) | collective-permute-done | bytes 196640 | tf_op jit(solution)/shard_map/ppermute | solution.py:29
  84.1 2.0 %collective-permute-done.26.d = bf16[96,1024]{1,0:T(8,128)(2,1)S(1)} collective-permute-done((bf16[96,1024]{1,0:T(8,128)(2,1)S(1)}, bf16[96,1024]{1,0:T(8,128)(2,1)S(1)}, u32[]{:S(2)}, u32[]{:S(2)}) %collective-permute-start.26) | collective-permute-done | bytes 196640 | tf_op jit(solution)/shard_map/ppermute | solution.py:29
  86.3 1.6 %collective-permute-start.28 = (bf16[24,1024]{1,0:T(8,128)(2,1)S(1)}, bf16[24,1024]{1,0:T(8,128)(2,1)S(1)}, u32[]{:S(2)}, u32[]{:S(2)}) collective-permute-start(bf16[24,1024]{1,0:T(8,128)(2,1)S(1)} %get-tuple-element.129), channel_id=1, source_target_pairs={{0,64},{1,65},{2,66},{3,67},{4,68},{5,69},{6,70},{7,71},{8,72},{9,... | collective-permute-start | bytes 147464 | tf_op jit(solution)/shard_map/ppermute | solution.py:29
  89.8 2.4 %collective-permute-done.28.c = bf16[24,1024]{1,0:T(8,128)(2,1)S(1)} collective-permute-done((bf16[24,1024]{1,0:T(8,128)(2,1)S(1)}, bf16[24,1024]{1,0:T(8,128)(2,1)S(1)}, u32[]{:S(2)}, u32[]{:S(2)}) %collective-permute-start.28) | collective-permute-done | bytes 49184 | tf_op jit(solution)/shard_map/ppermute | solution.py:29
  (61 shorter events, 25.4 us)
Async XLA Ops:
  1.9 5.7 %collective-permute-start = (bf16[24,1024]{1,0:T(8,128)(2,1)S(1)}, bf16[24,1024]{1,0:T(8,128)(2,1)S(1)}, u32[]{:S(2)}, u32[]{:S(2)}) collective-permute-start(bf16[24,1024]{1,0:T(8,128)(2,1)S(1)} %get-tuple-element.72), channel_id=1, source_target_pairs={{0,64},{1,65},{2,66},{3,67},{4,68},{5,69},{6,70},{7,71},{8,72},{9,... | collective-permute-start | bytes 147464 | tf_op jit(solution)/shard_map/ppermute | solution.py:29
  10.8 7.3 %collective-permute-start.3 = (bf16[96,1024]{1,0:T(8,128)(2,1)S(1)}, bf16[96,1024]{1,0:T(8,128)(2,1)S(1)}, u32[]{:S(2)}, u32[]{:S(2)}) collective-permute-start(bf16[96,1024]{1,0:T(8,128)(2,1)S(1)} %join_y.1.a), channel_id=1, source_target_pairs={{0,4},{1,17},{2,6},{3,19},{4,0},{5,21},{6,2},{7,23},{8,12},{9,25},... | collective-permute-start | bytes 589832 | tf_op jit(solution)/shard_map/ppermute | solution.py:29
  13.9 6.9 %collective-permute-start.4 = (bf16[96,1024]{1,0:T(8,128)(2,1)S(1)}, bf16[96,1024]{1,0:T(8,128)(2,1)S(1)}, u32[]{:S(2)}, u32[]{:S(2)}) collective-permute-start(bf16[96,1024]{1,0:T(8,128)(2,1)S(1)} %join_y.1.a), channel_id=1, source_target_pairs={{0,6},{1,25},{2,4},{3,27},{4,2},{5,29},{6,0},{7,31},{8,14},{9,17},... | collective-permute-start | bytes 589832 | tf_op jit(solution)/shard_map/ppermute | solution.py:29
  15.0 5.7 %collective-permute-start.5 = (bf16[96,1024]{1,0:T(8,128)(2,1)S(1)}, bf16[96,1024]{1,0:T(8,128)(2,1)S(1)}, u32[]{:S(2)}, u32[]{:S(2)}) collective-permute-start(bf16[96,1024]{1,0:T(8,128)(2,1)S(1)} %join_y.1.a), channel_id=1, source_target_pairs={{0,2},{1,9},{2,0},{3,11},{4,6},{5,13},{6,4},{7,15},{8,10},{9,1},{1... | collective-permute-start | bytes 589832 | tf_op jit(solution)/shard_map/ppermute | solution.py:29
  20.8 13.2 %collective-permute-start.6 = (bf16[4,48,1024]{2,1,0:T(8,128)(2,1)S(1)}, bf16[4,48,1024]{2,1,0:T(8,128)(2,1)S(1)}, u32[]{:S(2)}, u32[]{:S(2)}) collective-permute-start(bf16[4,48,1024]{2,1,0:T(8,128)(2,1)S(1)} %get-tuple-element.83.a), channel_id=1, source_target_pairs={{0,16},{1,5},{2,18},{3,7},{4,20},{5,1},{6,22},{7,3},{8,24},{9,13},... | collective-permute-start | bytes 1179656 | tf_op jit(solution)/shard_map/ppermute | solution.py:29
  24.8 10.0 %collective-permute-start.7 = (bf16[4,48,1024]{2,1,0:T(8,128)(2,1)S(1)}, bf16[4,48,1024]{2,1,0:T(8,128)(2,1)S(1)}, u32[]{:S(2)}, u32[]{:S(2)}) collective-permute-start(bf16[4,48,1024]{2,1,0:T(8,128)(2,1)S(1)} %get-tuple-element.83.a), channel_id=1, source_target_pairs={{0,24},{1,7},{2,26},{3,5},{4,28},{5,3},{6,30},{7,1},{8,16},{9,15},... | collective-permute-start | bytes 1179656 | tf_op jit(solution)/shard_map/ppermute | solution.py:29
  25.5 10.3 %collective-permute-start.8 = (bf16[4,48,1024]{2,1,0:T(8,128)(2,1)S(1)}, bf16[4,48,1024]{2,1,0:T(8,128)(2,1)S(1)}, u32[]{:S(2)}, u32[]{:S(2)}) collective-permute-start(bf16[4,48,1024]{2,1,0:T(8,128)(2,1)S(1)} %get-tuple-element.83.a), channel_id=1, source_target_pairs={{0,8},{1,3},{2,10},{3,1},{4,12},{5,7},{6,14},{7,5},{8,0},{9,11},{1... | collective-permute-start | bytes 1179656 | tf_op jit(solution)/shard_map/ppermute | solution.py:29
  25.8 13.7 %collective-permute-start.13 = (bf16[4,48,1024]{2,1,0:T(8,128)(2,1)S(1)}, bf16[4,48,1024]{2,1,0:T(8,128)(2,1)S(1)}, u32[]{:S(2)}, u32[]{:S(2)}) collective-permute-start(bf16[4,48,1024]{2,1,0:T(8,128)(2,1)S(1)} %get-tuple-element.90.a), channel_id=1, source_target_pairs={{0,16},{1,5},{2,18},{3,7},{4,20},{5,1},{6,22},{7,3},{8,24},{9,13},... | collective-permute-start | bytes 1179656 | tf_op jit(solution)/shard_map/ppermute | solution.py:29
  29.5 13.7 %collective-permute-start.14 = (bf16[4,48,1024]{2,1,0:T(8,128)(2,1)S(1)}, bf16[4,48,1024]{2,1,0:T(8,128)(2,1)S(1)}, u32[]{:S(2)}, u32[]{:S(2)}) collective-permute-start(bf16[4,48,1024]{2,1,0:T(8,128)(2,1)S(1)} %get-tuple-element.90.a), channel_id=1, source_target_pairs={{0,24},{1,7},{2,26},{3,5},{4,28},{5,3},{6,30},{7,1},{8,16},{9,15},... | collective-permute-start | bytes 1179656 | tf_op jit(solution)/shard_map/ppermute | solution.py:29
  34.0 10.3 %collective-permute-start.15 = (bf16[4,48,1024]{2,1,0:T(8,128)(2,1)S(1)}, bf16[4,48,1024]{2,1,0:T(8,128)(2,1)S(1)}, u32[]{:S(2)}, u32[]{:S(2)}) collective-permute-start(bf16[4,48,1024]{2,1,0:T(8,128)(2,1)S(1)} %get-tuple-element.90.a), channel_id=1, source_target_pairs={{0,8},{1,3},{2,10},{3,1},{4,12},{5,7},{6,14},{7,5},{8,0},{9,11},{1... | collective-permute-start | bytes 1179656 | tf_op jit(solution)/shard_map/ppermute | solution.py:29
  35.8 8.6 %collective-permute-start.9 = (bf16[4,48,1024]{2,1,0:T(8,128)(2,1)S(1)}, bf16[4,48,1024]{2,1,0:T(8,128)(2,1)S(1)}, u32[]{:S(2)}, u32[]{:S(2)}) collective-permute-start(bf16[4,48,1024]{2,1,0:T(8,128)(2,1)S(1)} %get-tuple-element.83.a), channel_id=1, source_target_pairs={{0,1},{1,0},{2,3},{3,2},{4,5},{5,4},{6,7},{7,6},{8,9},{9,8},{10,11... | collective-permute-start | bytes 1179656 | tf_op jit(solution)/shard_map/ppermute | solution.py:29
  35.8 8.6 %collective-permute-start.10 = (bf16[4,48,1024]{2,1,0:T(8,128)(2,1)S(1)}, bf16[4,48,1024]{2,1,0:T(8,128)(2,1)S(1)}, u32[]{:S(2)}, u32[]{:S(2)}) collective-permute-start(bf16[4,48,1024]{2,1,0:T(8,128)(2,1)S(1)} %collective-permute-done.6.c), channel_id=1, source_target_pairs={{0,1},{1,0},{2,3},{3,2},{4,5},{5,4},{6,7},{7,6},{8,9},{9,8},{10,11... | collective-permute-start | bytes 1179656 | tf_op jit(solution)/shard_map/ppermute | solution.py:29
  47.5 5.4 %collective-permute-start.21 = (bf16[4,4,48,1024]{3,2,1,0:T(8,128)(2,1)S(1)}, bf16[4,4,48,1024]{3,2,1,0:T(8,128)(2,1)S(1)}, u32[]{:S(2)}, u32[]{:S(2)}) collective-permute-start(bf16[4,4,48,1024]{3,2,1,0:T(8,128)(2,1)S(1)} %out_rows_1.1), channel_id=1, source_target_pairs={{0,1},{1,0},{2,3},{3,2},{4,5},{5,4},{6,7},{7,6},{8,9},{9,8},{10,11... | collective-permute-start | bytes 4718600 | tf_op jit(solution)/shard_map/ppermute | solution.py:29
  51.5 8.0 %collective-permute-start.17 = (bf16[4,4,48,1024]{3,2,1,0:T(8,128)(2,1)S(1)}, bf16[4,4,48,1024]{3,2,1,0:T(8,128)(2,1)S(1)}, u32[]{:S(2)}, u32[]{:S(2)}) collective-permute-start(bf16[4,4,48,1024]{3,2,1,0:T(8,128)(2,1)S(1)} %back_rows_1.1), channel_id=1, source_target_pairs={{0,1},{1,0},{2,3},{3,2},{4,5},{5,4},{6,7},{7,6},{8,9},{9,8},{10,11... | collective-permute-start | bytes 4718600 | tf_op jit(solution)/shard_map/ppermute | solution.py:29
  53.3 11.0 %collective-permute-start.22 = (bf16[4,48,1024]{2,1,0:T(8,128)(2,1)S(1)}, bf16[4,48,1024]{2,1,0:T(8,128)(2,1)S(1)}, u32[]{:S(2)}, u32[]{:S(2)}) collective-permute-start(bf16[4,48,1024]{2,1,0:T(8,128)(2,1)S(1)} %get-tuple-element.106), channel_id=1, source_target_pairs={{0,16},{1,5},{2,18},{3,7},{4,20},{5,1},{6,22},{7,3},{8,24},{9,13},... | collective-permute-start | bytes 1179656 | tf_op jit(solution)/shard_map/ppermute | solution.py:29
  57.9 13.4 %collective-permute-start.23 = (bf16[4,48,1024]{2,1,0:T(8,128)(2,1)S(1)}, bf16[4,48,1024]{2,1,0:T(8,128)(2,1)S(1)}, u32[]{:S(2)}, u32[]{:S(2)}) collective-permute-start(bf16[4,48,1024]{2,1,0:T(8,128)(2,1)S(1)} %get-tuple-element.107), channel_id=1, source_target_pairs={{0,24},{1,7},{2,26},{3,5},{4,28},{5,3},{6,30},{7,1},{8,16},{9,15},... | collective-permute-start | bytes 1179656 | tf_op jit(solution)/shard_map/ppermute | solution.py:29
  59.1 12.2 %collective-permute-start.24 = (bf16[4,48,1024]{2,1,0:T(8,128)(2,1)S(1)}, bf16[4,48,1024]{2,1,0:T(8,128)(2,1)S(1)}, u32[]{:S(2)}, u32[]{:S(2)}) collective-permute-start(bf16[4,48,1024]{2,1,0:T(8,128)(2,1)S(1)} %get-tuple-element.108), channel_id=1, source_target_pairs={{0,8},{1,3},{2,10},{3,1},{4,12},{5,7},{6,14},{7,5},{8,0},{9,11},{1... | collective-permute-start | bytes 1179656 | tf_op jit(solution)/shard_map/ppermute | solution.py:29
  59.9 12.9 %collective-permute-start.18 = (bf16[4,48,1024]{2,1,0:T(8,128)(2,1)S(1)}, bf16[4,48,1024]{2,1,0:T(8,128)(2,1)S(1)}, u32[]{:S(2)}, u32[]{:S(2)}) collective-permute-start(bf16[4,48,1024]{2,1,0:T(8,128)(2,1)S(1)} %get-tuple-element.101), channel_id=1, source_target_pairs={{0,16},{1,5},{2,18},{3,7},{4,20},{5,1},{6,22},{7,3},{8,24},{9,13},... | collective-permute-start | bytes 1179656 | tf_op jit(solution)/shard_map/ppermute | solution.py:29
  63.1 13.2 %collective-permute-start.19 = (bf16[4,48,1024]{2,1,0:T(8,128)(2,1)S(1)}, bf16[4,48,1024]{2,1,0:T(8,128)(2,1)S(1)}, u32[]{:S(2)}, u32[]{:S(2)}) collective-permute-start(bf16[4,48,1024]{2,1,0:T(8,128)(2,1)S(1)} %get-tuple-element.102), channel_id=1, source_target_pairs={{0,24},{1,7},{2,26},{3,5},{4,28},{5,3},{6,30},{7,1},{8,16},{9,15},... | collective-permute-start | bytes 1179656 | tf_op jit(solution)/shard_map/ppermute | solution.py:29
  64.2 12.1 %collective-permute-start.20 = (bf16[4,48,1024]{2,1,0:T(8,128)(2,1)S(1)}, bf16[4,48,1024]{2,1,0:T(8,128)(2,1)S(1)}, u32[]{:S(2)}, u32[]{:S(2)}) collective-permute-start(bf16[4,48,1024]{2,1,0:T(8,128)(2,1)S(1)} %get-tuple-element.103), channel_id=1, source_target_pairs={{0,8},{1,3},{2,10},{3,1},{4,12},{5,7},{6,14},{7,5},{8,0},{9,11},{1... | collective-permute-start | bytes 1179656 | tf_op jit(solution)/shard_map/ppermute | solution.py:29
  76.8 7.3 %collective-permute-start.25 = (bf16[96,1024]{1,0:T(8,128)(2,1)S(1)}, bf16[96,1024]{1,0:T(8,128)(2,1)S(1)}, u32[]{:S(2)}, u32[]{:S(2)}) collective-permute-start(bf16[96,1024]{1,0:T(8,128)(2,1)S(1)} %get-tuple-element.125), channel_id=1, source_target_pairs={{0,4},{1,17},{2,6},{3,19},{4,0},{5,21},{6,2},{7,23},{8,12},{9,25},... | collective-permute-start | bytes 589832 | tf_op jit(solution)/shard_map/ppermute | solution.py:29
  78.4 7.8 %collective-permute-start.26 = (bf16[96,1024]{1,0:T(8,128)(2,1)S(1)}, bf16[96,1024]{1,0:T(8,128)(2,1)S(1)}, u32[]{:S(2)}, u32[]{:S(2)}) collective-permute-start(bf16[96,1024]{1,0:T(8,128)(2,1)S(1)} %get-tuple-element.126), channel_id=1, source_target_pairs={{0,6},{1,25},{2,4},{3,27},{4,2},{5,29},{6,0},{7,31},{8,14},{9,17},... | collective-permute-start | bytes 589832 | tf_op jit(solution)/shard_map/ppermute | solution.py:29
  80.5 5.7 %collective-permute-start.27 = (bf16[96,1024]{1,0:T(8,128)(2,1)S(1)}, bf16[96,1024]{1,0:T(8,128)(2,1)S(1)}, u32[]{:S(2)}, u32[]{:S(2)}) collective-permute-start(bf16[96,1024]{1,0:T(8,128)(2,1)S(1)} %get-tuple-element.127), channel_id=1, source_target_pairs={{0,2},{1,9},{2,0},{3,11},{4,6},{5,13},{6,4},{7,15},{8,10},{9,1},{1... | collective-permute-start | bytes 589832 | tf_op jit(solution)/shard_map/ppermute | solution.py:29
  86.3 6.0 %collective-permute-start.28 = (bf16[24,1024]{1,0:T(8,128)(2,1)S(1)}, bf16[24,1024]{1,0:T(8,128)(2,1)S(1)}, u32[]{:S(2)}, u32[]{:S(2)}) collective-permute-start(bf16[24,1024]{1,0:T(8,128)(2,1)S(1)} %get-tuple-element.129), channel_id=1, source_target_pairs={{0,64},{1,65},{2,66},{3,67},{4,68},{5,69},{6,70},{7,71},{8,72},{9,... | collective-permute-start | bytes 147464 | tf_op jit(solution)/shard_map/ppermute | solution.py:29
  (7 other events, 29.9 us)
